TPU v7x, 32 devices: a whole 2x2x4 slice. The times are simulated.
32 devices in a mesh: narrow: 4 (over z), wide: 8 (over y, x, core).
Axes of the slice: x: 2, y: 2, z: 4, core: 2. Of those that a mesh axis runs over, the one named last changes fastest.
Arguments:
- tokens: bfloat16 [64, 512, 768], P(('narrow', 'wide')), may hold values from -6 to 6
- w_query: bfloat16 [768, 768], P(('narrow', 'wide')), may hold values from -0.109375 to 0.109375
- w_key: bfloat16 [768, 768], P(('narrow', 'wide')), may hold values from -0.109375 to 0.109375
- w_value: bfloat16 [768, 768], P(('narrow', 'wide')), may hold values from -0.21875 to 0.21875
- w_output: bfloat16 [768, 768], P(('narrow', 'wide')), may hold values from -0.625 to 0.625
- w_router: bfloat16 [768, 32], P(('narrow', 'wide')), may hold values from -0.15625 to 0.15625
- gain_attn: bfloat16 [768], P(('narrow', 'wide')), may hold values from 0.25 to 1.75
- gain_ffn: bfloat16 [768], P(('narrow', 'wide')), may hold values from 0.25 to 1.75
- rel_bias: bfloat16 [384], P(('narrow', 'wide')), may hold values from -4 to 4
- router_bias: bfloat16 [32], P(('narrow', 'wide')), may hold values from -0.59765625 to 0.59765625
- w_in: bfloat16 [32, 768, 3072], P(('narrow', 'wide')), may hold values from -0.21875 to 0.21875
- w_out: bfloat16 [32, 3072, 768], P(('narrow', 'wide')), may hold values from -4.96875 to 4.96875
- routes: int32 [64, 512, 1], P(('narrow', 'wide')), may hold values from 0 to 31
- fill_rank: int32 [64, 512], P(('narrow', 'wide')), may hold values from 0 to 511, each once within a row
- bucket_map: int32 [1023], replicated, may hold values from 0 to 31
- upstream_grad: bfloat16 [64, 512, 768], P(('narrow', 'wide')), may hold values from -6 to 6
Outputs:
- layer_out: bfloat16 [64, 512, 768], P(('narrow', 'wide'))
- grad_tokens: bfloat16 [64, 512, 768], P(('narrow', 'wide'))
- grad_query_w: float32 [768, 768], P(('narrow', 'wide'))
- grad_key_w: float32 [768, 768], P(('narrow', 'wide'))
- grad_value_w: float32 [768, 768], P(('narrow', 'wide'))
- grad_output_w: float32 [768, 768], P(('narrow', 'wide'))
- grad_router_w: float32 [768, 32], P(('narrow', 'wide'))
- grad_gain_attn: float32 [768], P(('narrow', 'wide'))
- grad_gain_ffn: float32 [768], P(('narrow', 'wide'))
- grad_rel_bias: float32 [384], P(('narrow', 'wide'))
- grad_router_bias: float32 [32], P(('narrow', 'wide'))
- grad_w_in: float32 [32, 768, 3072], P(('narrow', 'wide'))
- grad_w_out: float32 [32, 3072, 768], P(('narrow', 'wide'))
Inputs may be any that keep to these rules, and one draw needn't show every extreme that they name: `routes`: each token's single expert. `fill_rank`: in each sequence a permutation of 0 to 511.
All inputs are finite; a program needn't handle non-finite values.
Results may differ from a plain program's by a relative error of at most 0.025.
Values may be sent and summed in bfloat16 or wider, within the bound.
No kernel may reach another device: no remote copies, remote signals or barrier semaphores. Data moves between devices by JAX's collectives and lax.ppermute only.
A program may use at most 256 MiB of HBM per device.

v0:
```python
import jax
import jax.numpy as jnp
from jax import lax
from jax.sharding import PartitionSpec as P

HEADS = 12
HEAD = 64
BUCKETS = 32


epsilon = 1e-06


def for_sending(value):

    def short(part):
        return part.astype(jnp.bfloat16) if part.dtype == jnp.float32 else part

    return jax.tree.map(short, value)


def smooth_unit(values):
    return jax.nn.gelu(values, approximate=False)


def norm_forward(values, gain):
    scale = lax.rsqrt(jnp.mean(values * values, axis=-1, keepdims=True) + epsilon)
    return (values * scale * gain, scale)


def norm_backward(values, scale, gain, grad):
    weighted = grad * gain
    grad_values = scale * weighted - values * scale**3 * jnp.mean(
        weighted * values, axis=-1, keepdims=True
    )
    return (grad_values, jnp.sum(grad * values * scale, axis=0))


def send_rows(buffer):
    moved = lax.all_to_all(buffer, ("narrow", "wide"), split_axis=0, concat_axis=0, tiled=True)
    return moved


def return_rows(buffer):
    moved = lax.all_to_all(
        for_sending(buffer), ("narrow", "wide"), split_axis=0, concat_axis=0, tiled=True
    ).astype(buffer.dtype)
    return moved


def send_grads(buffer):
    moved = lax.all_to_all(buffer, ("narrow", "wide"), split_axis=0, concat_axis=0, tiled=True)
    return moved


def return_grads(buffer):
    moved = lax.all_to_all(
        for_sending(buffer), ("narrow", "wide"), split_axis=0, concat_axis=0, tiled=True
    ).astype(buffer.dtype)
    return moved


def reduce_grads(
    g_query, g_key, g_value, g_output, g_router, g_gain_one, g_gain_two, g_table, g_bias
):
    return (
        lax.psum_scatter(g_query, ("narrow", "wide"), scatter_dimension=0, tiled=True),
        lax.psum_scatter(g_key, ("narrow", "wide"), scatter_dimension=0, tiled=True),
        lax.psum_scatter(g_value, ("narrow", "wide"), scatter_dimension=0, tiled=True),
        lax.psum_scatter(g_output, ("narrow", "wide"), scatter_dimension=0, tiled=True),
        lax.psum_scatter(g_router, ("narrow", "wide"), scatter_dimension=0, tiled=True),
        lax.psum_scatter(g_gain_one, ("narrow", "wide"), scatter_dimension=0, tiled=True),
        lax.psum_scatter(g_gain_two, ("narrow", "wide"), scatter_dimension=0, tiled=True),
        lax.psum_scatter(g_table, ("narrow", "wide"), scatter_dimension=0, tiled=True),
        lax.psum_scatter(g_bias, ("narrow", "wide"), scatter_dimension=0, tiled=True),
    )


def body(
    tokens,
    w_query,
    w_key,
    w_value,
    w_output,
    w_router,
    gain_attn,
    gain_ffn,
    rel_bias,
    router_bias,
    w_in,
    w_out,
    routes,
    fill_rank,
    bucket_map,
    upstream_grad,
):
    batches, length, width = tokens.shape
    devices = lax.axis_size(("narrow", "wide"))
    local_experts = w_in.shape[0]
    experts = local_experts * devices
    capacity = max(2, 5 * length // (4 * experts))
    slots = experts * capacity
    places = jnp.arange(length, dtype=jnp.int32)
    distance = places[None, :] - places[:, None] + length - 1
    bucket_hot = (
        jnp.arange(BUCKETS, dtype=jnp.int32)[:, None] == bucket_map[distance].reshape(1, -1)
    ).astype(jnp.bfloat16)
    slot_ids = jnp.arange(slots, dtype=jnp.int32)
    expert_ids = jnp.arange(experts, dtype=jnp.int32)

    def one_batch(carry, inputs):
        shared, grad_in_sum, grad_out_sum = carry
        acts, route_col, order, upstream = inputs
        wq_all, wk_all, wv_all, wo_all, wr_all, gain_one, gain_two, rel_flat, bias_all = (
            lax.all_gather(w_query, ("narrow", "wide"), axis=0, tiled=True),
            lax.all_gather(w_key, ("narrow", "wide"), axis=0, tiled=True),
            lax.all_gather(w_value, ("narrow", "wide"), axis=0, tiled=True),
            lax.all_gather(w_output, ("narrow", "wide"), axis=0, tiled=True),
            lax.all_gather(w_router, ("narrow", "wide"), axis=0, tiled=True),
            lax.all_gather(gain_attn, ("narrow", "wide"), axis=0, tiled=True),
            lax.all_gather(gain_ffn, ("narrow", "wide"), axis=0, tiled=True),
            lax.all_gather(rel_bias, ("narrow", "wide"), axis=0, tiled=True),
            lax.all_gather(router_bias, ("narrow", "wide"), axis=0, tiled=True),
        )
        gain_one32 = gain_one.astype(jnp.float32)
        gain_two32 = gain_two.astype(jnp.float32)
        table = rel_flat.reshape(BUCKETS, HEADS).T
        acts32 = acts.astype(jnp.float32)
        normed, scale_one = norm_forward(acts32, gain_one32)
        normed_b = normed.astype(jnp.bfloat16)
        queries = (
            jnp.dot(normed_b, wq_all, preferred_element_type=jnp.float32)
            .astype(jnp.bfloat16)
            .reshape(length, HEADS, HEAD)
        )
        keys_all = (
            jnp.dot(normed_b, wk_all, preferred_element_type=jnp.float32)
            .astype(jnp.bfloat16)
            .reshape(length, HEADS, HEAD)
        )
        values = (
            jnp.dot(normed_b, wv_all, preferred_element_type=jnp.float32)
            .astype(jnp.bfloat16)
            .reshape(length, HEADS, HEAD)
        )
        bias = jnp.dot(table, bucket_hot, preferred_element_type=jnp.float32).reshape(
            HEADS, length, length
        )
        scores = (
            jnp.einsum("qhd,khd->hqk", queries, keys_all, preferred_element_type=jnp.float32) + bias
        )
        peak = jnp.max(scores, axis=-1, keepdims=True)
        total = jnp.log(jnp.sum(jnp.exp(scores - peak), axis=-1, keepdims=True)) + peak
        probs_b = jnp.exp(scores - total).astype(jnp.bfloat16)
        mixed = (
            jnp.einsum("hqk,khd->qhd", probs_b, values, preferred_element_type=jnp.float32)
            .astype(jnp.bfloat16)
            .reshape(length, width)
        )
        branch = jnp.dot(mixed, wo_all, preferred_element_type=jnp.float32)
        resid = acts32 + branch
        normed_two, scale_two = norm_forward(resid, gain_two32)
        normed_two_b = normed_two.astype(jnp.bfloat16)
        logits = jnp.dot(
            normed_two_b, wr_all, preferred_element_type=jnp.float32
        ) + bias_all.astype(jnp.float32)
        router_probs = jax.nn.softmax(logits, axis=-1)
        route = route_col[:, 0]
        route_hot = (route[:, None] == expert_ids[None, :]).astype(jnp.float32)
        gate = jnp.sum(router_probs * route_hot, axis=-1)
        earlier = (order[None, :] < order[:, None]).astype(jnp.bfloat16)
        counts = jnp.dot(
            earlier, route_hot.astype(jnp.bfloat16), preferred_element_type=jnp.float32
        )
        slot = jnp.sum(counts * route_hot, axis=-1).astype(jnp.int32)
        target = jnp.where(slot < capacity, route * capacity + slot, -1)
        sender = (slot_ids[:, None] == target[None, :]).astype(jnp.bfloat16)
        outgoing = jnp.dot(sender, normed_two_b, preferred_element_type=jnp.float32).astype(
            jnp.bfloat16
        )
        arrived = send_rows(outgoing.reshape(devices, local_experts * capacity, width)).reshape(
            devices, local_experts, capacity, width
        )
        rows_list, inner_list, active_list, result_list = ([], [], [], [])
        local = 0
        rows = arrived[:, local].reshape(devices * capacity, width)
        inner = jnp.dot(rows, w_in[local], preferred_element_type=jnp.float32)
        active = smooth_unit(inner).astype(jnp.bfloat16)
        result = jnp.dot(active, w_out[local], preferred_element_type=jnp.float32).astype(
            jnp.bfloat16
        )
        rows_list.append(rows)
        inner_list.append(inner)
        active_list.append(active)
        result_list.append(result.reshape(devices, capacity, width))
        produced = jnp.stack(result_list, axis=1).reshape(devices, local_experts * capacity, width)
        returned = return_rows(produced).reshape(slots, width)
        expert_rows = jnp.einsum("ct,cd->td", sender, returned, preferred_element_type=jnp.float32)
        output = (resid + gate[:, None] * expert_rows).astype(jnp.bfloat16)
        upstream32 = upstream.astype(jnp.float32)
        grad_gate = jnp.sum(upstream32 * expert_rows, axis=-1)
        scaled_up = (gate[:, None] * upstream32).astype(jnp.bfloat16)
        grad_sent = jnp.dot(sender, scaled_up, preferred_element_type=jnp.float32).astype(
            jnp.bfloat16
        )
        grad_arrived = send_grads(
            grad_sent.reshape(devices, local_experts * capacity, width)
        ).reshape(devices, local_experts, capacity, width)
        grad_rows_list, grad_in_list, grad_out_list = ([], [], [])
        local = 0
        grad_result = grad_arrived[:, local].reshape(devices * capacity, width)
        grad_out_list.append(
            jnp.einsum(
                "rf,rd->fd", active_list[local], grad_result, preferred_element_type=jnp.float32
            )
        )
        grad_active = jnp.einsum(
            "rd,fd->rf", grad_result, w_out[local], preferred_element_type=jnp.float32
        )
        unused, smooth_pull = jax.vjp(smooth_unit, inner_list[local])
        grad_inner = smooth_pull(grad_active)[0].astype(jnp.bfloat16)
        grad_in_list.append(
            jnp.einsum(
                "rd,rf->df", rows_list[local], grad_inner, preferred_element_type=jnp.float32
            )
        )
        grad_rows = jnp.einsum(
            "rf,df->rd", grad_inner, w_in[local], preferred_element_type=jnp.float32
        ).astype(jnp.bfloat16)
        grad_rows_list.append(grad_rows.reshape(devices, capacity, width))
        grad_produced = jnp.stack(grad_rows_list, axis=1).reshape(
            devices, local_experts * capacity, width
        )
        grad_back = return_grads(grad_produced).reshape(slots, width)
        grad_from_experts = jnp.einsum(
            "ct,cd->td", sender, grad_back, preferred_element_type=jnp.float32
        )
        grad_logits = (
            router_probs * (route_hot * grad_gate[:, None] - (gate * grad_gate)[:, None])
        ).astype(jnp.bfloat16)
        grad_router_bias = jnp.sum(grad_logits.astype(jnp.float32), axis=0)
        grad_router_w = jnp.einsum(
            "td,te->de", normed_two_b, grad_logits, preferred_element_type=jnp.float32
        )
        grad_normed_two = (
            jnp.einsum("te,de->td", grad_logits, wr_all, preferred_element_type=jnp.float32)
            + grad_from_experts
        )
        grad_resid_norm, grad_gain_two = norm_backward(
            resid, scale_two, gain_two32, grad_normed_two
        )
        grad_resid = upstream32 + grad_resid_norm
        grad_branch = grad_resid.astype(jnp.bfloat16)
        grad_output_w = jnp.einsum(
            "td,te->de", mixed, grad_branch, preferred_element_type=jnp.float32
        )
        grad_mixed = (
            jnp.einsum("te,de->td", grad_branch, wo_all, preferred_element_type=jnp.float32)
            .astype(jnp.bfloat16)
            .reshape(length, HEADS, HEAD)
        )
        again = (
            jnp.einsum("qhd,khd->hqk", queries, keys_all, preferred_element_type=jnp.float32) + bias
        )
        probs_again = jnp.exp(again - total)
        grad_probs = jnp.einsum(
            "qhd,khd->hqk", grad_mixed, values, preferred_element_type=jnp.float32
        )
        center = jnp.sum(probs_again * grad_probs, axis=-1, keepdims=True)
        grad_scores = (probs_again * (grad_probs - center)).astype(jnp.bfloat16)
        grad_values = (
            jnp.einsum(
                "hqk,qhd->khd",
                probs_again.astype(jnp.bfloat16),
                grad_mixed,
                preferred_element_type=jnp.float32,
            )
            .astype(jnp.bfloat16)
            .reshape(length, width)
        )
        grad_queries = (
            jnp.einsum("hqk,khd->qhd", grad_scores, keys_all, preferred_element_type=jnp.float32)
            .astype(jnp.bfloat16)
            .reshape(length, width)
        )
        grad_keys = (
            jnp.einsum("hqk,qhd->khd", grad_scores, queries, preferred_element_type=jnp.float32)
            .astype(jnp.bfloat16)
            .reshape(length, width)
        )
        grad_table = jnp.einsum(
            "hn,bn->hb",
            grad_scores.reshape(HEADS, length * length),
            bucket_hot,
            preferred_element_type=jnp.float32,
        )
        grad_rel = grad_table.T.reshape(-1)
        grad_query_w = jnp.einsum(
            "td,te->de", normed_b, grad_queries, preferred_element_type=jnp.float32
        )
        grad_key_w = jnp.einsum(
            "td,te->de", normed_b, grad_keys, preferred_element_type=jnp.float32
        )
        grad_value_w = jnp.einsum(
            "td,te->de", normed_b, grad_values, preferred_element_type=jnp.float32
        )
        grad_normed = jnp.einsum(
            "te,de->td", grad_queries, wq_all, preferred_element_type=jnp.float32
        )
        grad_normed = grad_normed + jnp.einsum(
            "te,de->td", grad_keys, wk_all, preferred_element_type=jnp.float32
        )
        grad_normed = grad_normed + jnp.einsum(
            "te,de->td", grad_values, wv_all, preferred_element_type=jnp.float32
        )
        grad_acts_norm, grad_gain_one = norm_backward(acts32, scale_one, gain_one32, grad_normed)
        grad_acts = (grad_resid + grad_acts_norm).astype(jnp.bfloat16)
        update = reduce_grads(
            grad_query_w,
            grad_key_w,
            grad_value_w,
            grad_output_w,
            grad_router_w,
            grad_gain_one,
            grad_gain_two,
            grad_rel,
            grad_router_bias,
        )
        shared = tuple((older + newer for older, newer in zip(shared, update)))
        grad_in_sum = grad_in_sum + jnp.stack(grad_in_list, axis=0)
        grad_out_sum = grad_out_sum + jnp.stack(grad_out_list, axis=0)
        return ((shared, grad_in_sum, grad_out_sum), (output, grad_acts))

    start = tuple(
        (
            jnp.zeros(member.shape, jnp.float32)
            for member in (
                w_query,
                w_key,
                w_value,
                w_output,
                w_router,
                gain_attn,
                gain_ffn,
                rel_bias,
                router_bias,
            )
        )
    )
    initial = (start, jnp.zeros(w_in.shape, jnp.float32), jnp.zeros(w_out.shape, jnp.float32))
    (shared, grad_in_sum, grad_out_sum), (outputs, grad_inputs) = lax.scan(
        one_batch, initial, (tokens, routes, fill_rank, upstream_grad)
    )
    return (
        outputs,
        grad_inputs,
        shared[0],
        shared[1],
        shared[2],
        shared[3],
        shared[4],
        shared[5],
        shared[6],
        shared[7],
        shared[8],
        grad_in_sum,
        grad_out_sum,
    )


def solution(mesh):
    in_specs = (
        P(("narrow", "wide"), None, None),
        P(("narrow", "wide"), None),
        P(("narrow", "wide"), None),
        P(("narrow", "wide"), None),
        P(("narrow", "wide"), None),
        P(("narrow", "wide"), None),
        P(("narrow", "wide")),
        P(("narrow", "wide")),
        P(("narrow", "wide")),
        P(("narrow", "wide")),
        P(("narrow", "wide"), None, None),
        P(("narrow", "wide"), None, None),
        P(("narrow", "wide"), None, None),
        P(("narrow", "wide"), None),
        P(),
        P(("narrow", "wide"), None, None),
    )
    out_specs = (
        P(("narrow", "wide"), None, None),
        P(("narrow", "wide"), None, None),
        P(("narrow", "wide"), None),
        P(("narrow", "wide"), None),
        P(("narrow", "wide"), None),
        P(("narrow", "wide"), None),
        P(("narrow", "wide"), None),
        P(("narrow", "wide")),
        P(("narrow", "wide")),
        P(("narrow", "wide")),
        P(("narrow", "wide")),
        P(("narrow", "wide"), None, None),
        P(("narrow", "wide"), None, None),
    )
    return jax.shard_map(body, mesh=mesh, in_specs=in_specs, out_specs=out_specs, check_vma=False)
```

profile of v0, /device:TPU:0, one launch (start us, length us, event | category | flops | bytes accessed | tf_op | source)
XLA Modules:
  0.0 2925.0 jit_solution(13577079181894826623)
XLA Ops:
  8.1 42.0 %all-reduce.3 = bf16[384]{0:T(512)(128)(2,1)S(1)} all-reduce(bf16[384]{0:T(512)(128)(2,1)S(1)} %dynamic-update-slice.3), channel_id=1, replica_groups=mesh['narrow'=4,'wide'=8] {'narrow','wide'}, use_global_device_ids=true, to_apply=%add.3 | all-reduce | flops 384 | bytes 1536
  51.4 1041.2 %gather_fusion = s32[262144]{0:T(1024)S(1)} fusion(s32[1023]{0:T(1024)S(1)} %copy-done, s32[262144]{0:T(1024)S(1)} %broadcast_clamp_fusion), kind=kCustom, calls=%fused_computation | custom fusion | bytes 3145728 | tf_op jit(solution)/shard_map/gather | solution.py:106
  1123.1 1793.0 %while.37 = (s32[]{:T(128)}, f32[24,768]{1,0:T(8,128)}, f32[24,768]{1,0:T(8,128)}, f32[24,768]{1,0:T(8,128)}, f32[24,768]{1,0:T(8,128)}, /*index=5*/f32[24,32]{1...) while((s32[]{:T(128)}, f32[24,768]{1,0:T(8,128)}, ...), condition=%wide.region_25.26_spmd.clone, body=%wide.region_0.25_spmd.clone.sunk | while | flops 30355761152 | bytes 701685376 | solution.py:351
  1130.6 40.3 %all-reduce.16 = (bf16[768]{0:T(1024)(128)(2,1)S(1)}, bf16[768]{0:T(1024)(128)(2,1)S(1)}, bf16[32]{0:T(256)(128)(2,1)S(1)}) all-reduce(bf16[768]{0:T(1024)(128)(2,1)S(1)} %dynamic-update-slice.10, bf16[768]{0:T(1024)(128)(2,1)S(1)} %dynamic-update-slice.11, ...), channel_id=1, replica_groups=mesh['narrow'=4,'wide'=8] {'narrow','wide'}, use_global_device_ids=true, to_apply=%add | all-reduce | flops 1568 | bytes 6272 | tf_op jit(solution)/shard_map/while
  1183.4 53.5 %all-gather.7.cloned.1.call-done = bf16[768,768]{1,0:T(8,128)(2,1)} async-done(((bf16[24,768]{1,0:T(8,128)(2,1)}), bf16[768,768]{1,0:T(8,128)(2,1)}) %all-gather.7.cloned.1.call-update) | async-done | bytes 1179664 | tf_op jit(solution)/shard_map/while/body/eval_jaxpr/all_gather | solution.py:115
  1240.2 52.6 %all-gather.5.cloned.1.call-done = bf16[768,768]{1,0:T(8,128)(2,1)} async-done(((bf16[24,768]{1,0:T(8,128)(2,1)}), bf16[768,768]{1,0:T(8,128)(2,1)}) %all-gather.5.cloned.1.call-update) | async-done | bytes 1179664 | tf_op jit(solution)/shard_map/while/body/eval_jaxpr/all_gather | solution.py:116
  1311.7 36.8 %all-gather.9.cloned.1.call-done = bf16[768,768]{1,0:T(8,128)(2,1)} async-done(((bf16[24,768]{1,0:T(8,128)(2,1)}), bf16[768,768]{1,0:T(8,128)(2,1)}) %all-gather.9.cloned.1.call-update) | async-done | bytes 1179664 | tf_op jit(solution)/shard_map/while/body/eval_jaxpr/all_gather | solution.py:118
  1359.6 54.9 %all_gather.60 = bf16[768,32]{1,0:T(8,128)(2,1)S(1)} all-gather(bf16[24,32]{1,0:T(8,128)(2,1)S(1)} %get-tuple-element.1029), channel_id=1, replica_groups=mesh['narrow'=4,'wide'=8] {'narrow','wide'}, dimensions={0}, use_global_device_ids=true | all-gather | bytes 50688 | tf_op jit(solution)/shard_map/while/body/eval_jaxpr/all_gather | solution.py:119
  1426.7 22.4 multiply_convert_fusion.7
  1508.8 19.3 all-to-all-done.3
  1644.9 38.5 %all-reduce.17 = (f32[768]{0:T(1024)S(1)}, f32[768]{0:T(1024)S(1)}, f32[384]{0:T(512)S(1)}, f32[32]{0:T(128)S(1)}) all-reduce(f32[768]{0:T(1024)S(1)} %get-tuple-element.917, f32[768]{0:T(1024)S(1)} %get-tuple-element.918, f32[384]{0:T(512)S(1)} %reshape.381, ...), channel_id=7, replica_groups=mesh['narrow'=4,'wide'=8] {'narrow','wide'}, use_global_device_ids=true, to_apply=%region_18.18.clone | all-reduce | flops 1952 | bytes 15616 | tf_op jit(solution)/shard_map/while
  1708.5 102.4 %reduce-scatter.14.cloned.1.call-done = f32[24,768]{1,0:T(8,128)} async-done(((f32[768,768]{1,0:T(8,128)}), f32[24,768]{1,0:T(8,128)}) %reduce-scatter.14.cloned.1.call-update) | async-done | bytes 73744 | tf_op jit(solution)/shard_map/while/body/eval_jaxpr/reduce_scatter | solution.py:69
  1811.8 103.3 %reduce-scatter.12.cloned.1.call-done = f32[24,768]{1,0:T(8,128)} async-done(((f32[768,768]{1,0:T(8,128)}), f32[24,768]{1,0:T(8,128)}) %reduce-scatter.12.cloned.1.call-update) | async-done | bytes 73744 | tf_op jit(solution)/shard_map/while/body/eval_jaxpr/reduce_scatter | solution.py:68
  1916.0 102.5 %reduce-scatter.10.cloned.1.call-done = f32[24,768]{1,0:T(8,128)} async-done(((f32[768,768]{1,0:T(8,128)}), f32[24,768]{1,0:T(8,128)}) %reduce-scatter.10.cloned.1.call-update) | async-done | bytes 73744 | tf_op jit(solution)/shard_map/while/body/eval_jaxpr/reduce_scatter | solution.py:67
  2027.3 40.3 %all-reduce.16 = (bf16[768]{0:T(1024)(128)(2,1)S(1)}, bf16[768]{0:T(1024)(128)(2,1)S(1)}, bf16[32]{0:T(256)(128)(2,1)S(1)}) all-reduce(bf16[768]{0:T(1024)(128)(2,1)S(1)} %dynamic-update-slice.10, bf16[768]{0:T(1024)(128)(2,1)S(1)} %dynamic-update-slice.11, ...), channel_id=1, replica_groups=mesh['narrow'=4,'wide'=8] {'narrow','wide'}, use_global_device_ids=true, to_apply=%add | all-reduce | flops 1568 | bytes 6272 | tf_op jit(solution)/shard_map/while
  2079.1 53.7 %all-gather.7.cloned.1.call-done = bf16[768,768]{1,0:T(8,128)(2,1)} async-done(((bf16[24,768]{1,0:T(8,128)(2,1)}), bf16[768,768]{1,0:T(8,128)(2,1)}) %all-gather.7.cloned.1.call-update) | async-done | bytes 1179664 | tf_op jit(solution)/shard_map/while/body/eval_jaxpr/all_gather | solution.py:115
  2136.1 52.5 %all-gather.5.cloned.1.call-done = bf16[768,768]{1,0:T(8,128)(2,1)} async-done(((bf16[24,768]{1,0:T(8,128)(2,1)}), bf16[768,768]{1,0:T(8,128)(2,1)}) %all-gather.5.cloned.1.call-update) | async-done | bytes 1179664 | tf_op jit(solution)/shard_map/while/body/eval_jaxpr/all_gather | solution.py:116
  2207.5 37.0 %all-gather.9.cloned.1.call-done = bf16[768,768]{1,0:T(8,128)(2,1)} async-done(((bf16[24,768]{1,0:T(8,128)(2,1)}), bf16[768,768]{1,0:T(8,128)(2,1)}) %all-gather.9.cloned.1.call-update) | async-done | bytes 1179664 | tf_op jit(solution)/shard_map/while/body/eval_jaxpr/all_gather | solution.py:118
  2255.5 54.9 %all_gather.60 = bf16[768,32]{1,0:T(8,128)(2,1)S(1)} all-gather(bf16[24,32]{1,0:T(8,128)(2,1)S(1)} %get-tuple-element.1029), channel_id=1, replica_groups=mesh['narrow'=4,'wide'=8] {'narrow','wide'}, dimensions={0}, use_global_device_ids=true | all-gather | bytes 50688 | tf_op jit(solution)/shard_map/while/body/eval_jaxpr/all_gather | solution.py:119
  2322.6 22.4 multiply_convert_fusion.7
  2545.8 38.6 %all-reduce.17 = (f32[768]{0:T(1024)S(1)}, f32[768]{0:T(1024)S(1)}, f32[384]{0:T(512)S(1)}, f32[32]{0:T(128)S(1)}) all-reduce(f32[768]{0:T(1024)S(1)} %get-tuple-element.917, f32[768]{0:T(1024)S(1)} %get-tuple-element.918, f32[384]{0:T(512)S(1)} %reshape.381, ...), channel_id=7, replica_groups=mesh['narrow'=4,'wide'=8] {'narrow','wide'}, use_global_device_ids=true, to_apply=%region_18.18.clone | all-reduce | flops 1952 | bytes 15616 | tf_op jit(solution)/shard_map/while
  2604.0 102.3 %reduce-scatter.14.cloned.1.call-done = f32[24,768]{1,0:T(8,128)} async-done(((f32[768,768]{1,0:T(8,128)}), f32[24,768]{1,0:T(8,128)}) %reduce-scatter.14.cloned.1.call-update) | async-done | bytes 73744 | tf_op jit(solution)/shard_map/while/body/eval_jaxpr/reduce_scatter | solution.py:69
  2707.2 103.1 %reduce-scatter.12.cloned.1.call-done = f32[24,768]{1,0:T(8,128)} async-done(((f32[768,768]{1,0:T(8,128)}), f32[24,768]{1,0:T(8,128)}) %reduce-scatter.12.cloned.1.call-update) | async-done | bytes 73744 | tf_op jit(solution)/shard_map/while/body/eval_jaxpr/reduce_scatter | solution.py:68
  2811.2 102.3 %reduce-scatter.10.cloned.1.call-done = f32[24,768]{1,0:T(8,128)} async-done(((f32[768,768]{1,0:T(8,128)}), f32[24,768]{1,0:T(8,128)}) %reduce-scatter.10.cloned.1.call-update) | async-done | bytes 73744 | tf_op jit(solution)/shard_map/while/body/eval_jaxpr/reduce_scatter | solution.py:67
  (430 shorter events, 587.9 us)
Async XLA Ops:
  1123.3 57.6 %all-gather.11.cloned.1.call-start = ((), (), s32[]{:S(2)}) async-start(), calls=%async_computation.12 | async-start | bytes 1216512 | tf_op jit(solution)/shard_map/while/body/eval_jaxpr/all_gather | solution.py:117
  1124.1 112.8 %all-gather.7.cloned.1.call-start = ((), (), s32[]{:S(2)}) async-start(), calls=%async_computation.10 | async-start | bytes 1216512 | tf_op jit(solution)/shard_map/while/body/eval_jaxpr/all_gather | solution.py:115
  1124.8 168.0 %all-gather.5.cloned.1.call-start = ((), (), s32[]{:S(2)}) async-start(), calls=%async_computation.9 | async-start | bytes 1216512 | tf_op jit(solution)/shard_map/while/body/eval_jaxpr/all_gather | solution.py:116
  1125.5 223.0 %all-gather.9.cloned.1.call-start = ((), (), s32[]{:S(2)}) async-start(), calls=%async_computation.11 | async-start | bytes 1216512 | tf_op jit(solution)/shard_map/while/body/eval_jaxpr/all_gather | solution.py:118
  1356.0 65.2 %all-to-all-start = ((bf16[32,20,768]{2,1,0:T(8,128)(2,1)}), bf16[32,20,768]{2,1,0:T(8,128)(2,1)}, u32[]{:S(2)}, u32[]{:S(2)}) async-start(bf16[32,20,768]{2,1,0:T(8,128)(2,1)} %reshape.373), calls=%async_computation | async-start | bytes 2359296 | tf_op jit(solution)/shard_map/while/body/eval_jaxpr/all_to_all | solution.py:40
  1421.2 38.5 %all-to-all-start.2 = ((bf16[32,20,768]{2,1,0:T(8,128)(2,1)}), bf16[32,20,768]{2,1,0:T(8,128)(2,1)}, u32[]{:S(2)}, u32[]{:S(2)}) async-start(bf16[32,20,768]{2,1,0:T(8,128)(2,1)} %reshape.377), calls=%async_computation.2 | async-start | bytes 2359296 | tf_op jit(solution)/shard_map/while/body/eval_jaxpr/all_to_all | solution.py:52
  1459.7 35.5 %all-to-all-start.1 = ((bf16[32,20,768]{2,1,0:T(8,128)(2,1)}), bf16[32,20,768]{2,1,0:T(8,128)(2,1)}, u32[]{:S(2)}, u32[]{:S(2)}) async-start(bf16[32,20,768]{2,1,0:T(8,128)(2,1)} %reshape.375), calls=%async_computation.1 | async-start | bytes 2359296 | tf_op jit(solution)/shard_map/while/body/eval_jaxpr/all_to_all | solution.py:45
  1499.0 190.5 %reduce-scatter.18.cloned.1.call-start = ((), (), s32[]{:S(2)}) async-start(), calls=%async_computation.17 | async-start | bytes 405504 | tf_op jit(solution)/shard_map/while
  1507.1 200.4 %reduce-scatter.16.cloned.1.call-start = ((), (), s32[]{:S(2)}) async-start(), calls=%async_computation.16 | async-start | bytes 2433024 | tf_op jit(solution)/shard_map/while/body/eval_jaxpr/reduce_scatter | solution.py:70
  1537.1 273.7 %reduce-scatter.14.cloned.1.call-start = ((), (), s32[]{:S(2)}) async-start(), calls=%async_computation.15 | async-start | bytes 2433024 | tf_op jit(solution)/shard_map/while/body/eval_jaxpr/reduce_scatter | solution.py:69
  1553.5 361.6 %reduce-scatter.12.cloned.1.call-start = ((), (), s32[]{:S(2)}) async-start(), calls=%async_computation.14 | async-start | bytes 2433024 | tf_op jit(solution)/shard_map/while/body/eval_jaxpr/reduce_scatter | solution.py:68
  1578.8 439.7 %reduce-scatter.10.cloned.1.call-start = ((), (), s32[]{:S(2)}) async-start(), calls=%async_computation.13 | async-start | bytes 2433024 | tf_op jit(solution)/shard_map/while/body/eval_jaxpr/reduce_scatter | solution.py:67
  2020.2 56.5 %all-gather.11.cloned.1.call-start = ((), (), s32[]{:S(2)}) async-start(), calls=%async_computation.12 | async-start | bytes 1216512 | tf_op jit(solution)/shard_map/while/body/eval_jaxpr/all_gather | solution.py:117
  2020.8 112.0 %all-gather.7.cloned.1.call-start = ((), (), s32[]{:S(2)}) async-start(), calls=%async_computation.10 | async-start | bytes 1216512 | tf_op jit(solution)/shard_map/while/body/eval_jaxpr/all_gather | solution.py:115
  2021.5 167.0 %all-gather.5.cloned.1.call-start = ((), (), s32[]{:S(2)}) async-start(), calls=%async_computation.9 | async-start | bytes 1216512 | tf_op jit(solution)/shard_map/while/body/eval_jaxpr/all_gather | solution.py:116
  2022.1 222.4 %all-gather.9.cloned.1.call-start = ((), (), s32[]{:S(2)}) async-start(), calls=%async_computation.11 | async-start | bytes 1216512 | tf_op jit(solution)/shard_map/while/body/eval_jaxpr/all_gather | solution.py:118
  2251.9 65.2 %all-to-all-start = ((bf16[32,20,768]{2,1,0:T(8,128)(2,1)}), bf16[32,20,768]{2,1,0:T(8,128)(2,1)}, u32[]{:S(2)}, u32[]{:S(2)}) async-start(bf16[32,20,768]{2,1,0:T(8,128)(2,1)} %reshape.373), calls=%async_computation | async-start | bytes 2359296 | tf_op jit(solution)/shard_map/while/body/eval_jaxpr/all_to_all | solution.py:40
  2317.1 38.5 %all-to-all-start.2 = ((bf16[32,20,768]{2,1,0:T(8,128)(2,1)}), bf16[32,20,768]{2,1,0:T(8,128)(2,1)}, u32[]{:S(2)}, u32[]{:S(2)}) async-start(bf16[32,20,768]{2,1,0:T(8,128)(2,1)} %reshape.377), calls=%async_computation.2 | async-start | bytes 2359296 | tf_op jit(solution)/shard_map/while/body/eval_jaxpr/all_to_all | solution.py:52
  2355.6 35.3 %all-to-all-start.1 = ((bf16[32,20,768]{2,1,0:T(8,128)(2,1)}), bf16[32,20,768]{2,1,0:T(8,128)(2,1)}, u32[]{:S(2)}, u32[]{:S(2)}) async-start(bf16[32,20,768]{2,1,0:T(8,128)(2,1)} %reshape.375), calls=%async_computation.1 | async-start | bytes 2359296 | tf_op jit(solution)/shard_map/while/body/eval_jaxpr/all_to_all | solution.py:45
  2394.7 195.7 %reduce-scatter.18.cloned.1.call-start = ((), (), s32[]{:S(2)}) async-start(), calls=%async_computation.17 | async-start | bytes 405504 | tf_op jit(solution)/shard_map/while
  2402.8 200.3 %reduce-scatter.16.cloned.1.call-start = ((), (), s32[]{:S(2)}) async-start(), calls=%async_computation.16 | async-start | bytes 2433024 | tf_op jit(solution)/shard_map/while/body/eval_jaxpr/reduce_scatter | solution.py:70
  2432.8 273.4 %reduce-scatter.14.cloned.1.call-start = ((), (), s32[]{:S(2)}) async-start(), calls=%async_computation.15 | async-start | bytes 2433024 | tf_op jit(solution)/shard_map/while/body/eval_jaxpr/reduce_scatter | solution.py:69
  2449.2 361.1 %reduce-scatter.12.cloned.1.call-start = ((), (), s32[]{:S(2)}) async-start(), calls=%async_computation.14 | async-start | bytes 2433024 | tf_op jit(solution)/shard_map/while/body/eval_jaxpr/reduce_scatter | solution.py:68
  2474.5 439.1 %reduce-scatter.10.cloned.1.call-start = ((), (), s32[]{:S(2)}) async-start(), calls=%async_computation.13 | async-start | bytes 2433024 | tf_op jit(solution)/shard_map/while/body/eval_jaxpr/reduce_scatter | solution.py:67
  (92 other events, 4985.4 us)
Sparse Core Ops, SparseCore 0:
  1127.1 53.8 all-gather.10
  1183.8 53.0 all-gather.6
  1239.8 52.9 all-gather.4
  1295.5 52.9 all-gather.8
  1507.2 95.9 reduce-scatter.17
  1609.2 98.2 reduce-scatter.15
  1712.8 98.0 reduce-scatter.13
  1817.0 98.0 reduce-scatter.11
  1920.4 98.0 reduce-scatter.9
  2023.6 53.0 all-gather.10
  2079.6 53.1 all-gather.6
  2135.5 52.9 all-gather.4
  2191.4 52.9 all-gather.8
  2402.9 95.9 reduce-scatter.17
  2504.9 98.1 reduce-scatter.15
  2608.2 98.0 reduce-scatter.13
  2712.3 97.9 reduce-scatter.11
  2815.4 98.0 reduce-scatter.9
where the time goes:
time: 2930 us
  local copies, waits for them, and re-layouts  1190 us (41%)
  waiting for transfers between devices  1000 us (34%)
  matrix products  317 us (11%)
  blocking collectives  309 us (11%)
  other arithmetic  43.4 us (1%)
  starting transfers between devices  35.4 us (1%)
    gather x1, local copies, waits for them, and re-layouts, body(): bucket_map[distance].reshape(1, -1)  1040 us
    reduce_scatter x2, waiting for transfers between devices, reduce_grads(): lax.psum_scatter(g_key, ('narrow', 'wide'), scatter_dimension=0, tiled=True)  206 us
    reduce_scatter x2, waiting for transfers between devices, reduce_grads(): lax.psum_scatter(g_query, ('narrow', 'wide'), scatter_dimension=0, tiled=...  205 us
    reduce_scatter x2, waiting for transfers between devices, reduce_grads(): lax.psum_scatter(g_value, ('narrow', 'wide'), scatter_dimension=0, tiled=...  205 us
    while x4, blocking collectives  158 us
    all_gather x2, blocking collectives, one_batch(): lax.all_gather(w_router, ('narrow', 'wide'), axis=0, tiled=True)  110 us
    all_gather x2, waiting for transfers between devices, one_batch(): lax.all_gather(w_query, ('narrow', 'wide'), axis=0, tiled=True)  107 us
    all_gather x2, waiting for transfers between devices, one_batch(): lax.all_gather(w_key, ('narrow', 'wide'), axis=0, tiled=True)  105 us
  transfers between devices with their start and end apart: 26, of which 20 were waited for; matrix products, arithmetic and copies ran while one was open for 15% of the time, Pallas kernels for 0%

commit v1 on v0

v1 whole, which is shorter than its diff:
```python
import jax
import jax.numpy as jnp
from jax import lax
from jax.experimental import pallas as pl
from jax.experimental.pallas import tpu as pltpu
from jax.sharding import PartitionSpec as P

HEADS = 12
HEAD = 64
BUCKETS = 32
AXES = ("narrow", "wide")

epsilon = 1e-06
f32 = jnp.float32
bf16 = jnp.bfloat16


def smooth_unit(values):
    return jax.nn.gelu(values, approximate=False)


def norm_forward(values, gain):
    scale = lax.rsqrt(jnp.mean(values * values, axis=-1, keepdims=True) + epsilon)
    return (values * scale * gain, scale)


def norm_backward(values, scale, gain, grad):
    weighted = grad * gain
    grad_values = scale * weighted - values * scale**3 * jnp.mean(
        weighted * values, axis=-1, keepdims=True
    )
    return (grad_values, jnp.sum(grad * values * scale, axis=0))


def exchange(buffer):
    return lax.all_to_all(buffer, AXES, split_axis=0, concat_axis=0, tiled=True)


def pack_rows(parts, width):
    lead = parts[0].shape[0]
    flat = jnp.concatenate([part.reshape(lead, -1) for part in parts], axis=1)
    short = -flat.shape[1] % width
    return jnp.pad(flat, ((0, 0), (0, short))).reshape(lead, -1, width)


def unpack_rows(packed, sizes):
    flat = packed.reshape(packed.shape[0], -1)
    out, at = [], 0
    for size in sizes:
        out.append(flat[:, at : at + size])
        at += size
    return out


def skew_kernel(lines_ref, out_ref):
    heads, block, span = out_ref.shape
    for head in range(heads):
        row = jnp.broadcast_to(lines_ref[head : head + 1, :], (block, span))
        out_ref[head] = pltpu.roll(row, span - (block - 1), 1, stride=1, stride_axis=0)


def skew_bias(lines, block):
    heads, span = lines.shape
    return pl.pallas_call(
        skew_kernel,
        out_shape=jax.ShapeDtypeStruct((heads, block, span), f32),
    )(lines)


def body(
    tokens,
    w_query,
    w_key,
    w_value,
    w_output,
    w_router,
    gain_attn,
    gain_ffn,
    rel_bias,
    router_bias,
    w_in,
    w_out,
    routes,
    fill_rank,
    bucket_map,
    upstream_grad,
):
    batches, length, width = tokens.shape
    devices = lax.axis_size(AXES)
    narrow = lax.axis_size("narrow")
    wide = lax.axis_size("wide")
    local_experts = w_in.shape[0]
    experts = local_experts * devices
    capacity = max(2, 5 * length // (4 * experts))
    slots = experts * capacity
    slot_ids = jnp.arange(slots, dtype=jnp.int32)
    expert_ids = jnp.arange(experts, dtype=jnp.int32)
    block = 128
    blocks = length // block
    span = 2 * length

    small_parts = [w_router, gain_attn, gain_ffn, rel_bias, router_bias]
    small = pack_rows([part.reshape(1, -1) for part in small_parts], width)[0]
    square = jnp.concatenate([w_query, w_key, w_value, w_output, small], axis=0)
    shard = w_query.shape[0]
    everything = lax.all_gather(square, AXES, axis=0)
    wq_all, wk_all, wv_all, wo_all = (
        everything[:, i * shard : (i + 1) * shard].reshape(width, width) for i in range(4)
    )
    wr_all, gain_one, gain_two, rel_flat, bias_all = unpack_rows(
        everything[:, 4 * shard :], [part.size for part in small_parts]
    )
    wr_all = wr_all.reshape(width, experts)
    gain_one32 = gain_one.reshape(-1).astype(f32)
    gain_two32 = gain_two.reshape(-1).astype(f32)
    bias_all32 = bias_all.reshape(-1).astype(f32)
    table = rel_flat.reshape(BUCKETS, HEADS).T

    bucket_hot = (
        jnp.arange(BUCKETS, dtype=jnp.int32)[:, None]
        == jnp.pad(bucket_map, (0, 1), constant_values=-1)[None, :]
    ).astype(bf16)
    lines = jnp.dot(table, bucket_hot, preferred_element_type=f32)
    skewed = skew_bias(lines, block)
    bias = jnp.concatenate(
        [
            skewed[:, :, length - block * (at + 1) : 2 * length - block * (at + 1)]
            for at in range(blocks)
        ],
        axis=1,
    )

    def plan(at):
        route = routes[at, :, 0]
        order = fill_rank[at]
        route_hot = (route[:, None] == expert_ids[None, :]).astype(f32)
        earlier = (order[None, :] < order[:, None]).astype(bf16)
        counts = jnp.dot(earlier, route_hot.astype(bf16), preferred_element_type=f32)
        slot = jnp.sum(counts * route_hot, axis=-1).astype(jnp.int32)
        target = jnp.where(slot < capacity, route * capacity + slot, -1)
        sender = (slot_ids[:, None] == target[None, :]).astype(bf16)
        return route_hot, sender

    def dispatch(sender, rows):
        moved = jnp.dot(sender, rows, preferred_element_type=f32).astype(bf16)
        return exchange(moved.reshape(devices, local_experts * capacity, width))

    def front(at):
        acts32 = tokens[at].astype(f32)
        normed, scale_one = norm_forward(acts32, gain_one32)
        normed_b = normed.astype(bf16)

        def project(weight):
            return (
                jnp.dot(normed_b, weight, preferred_element_type=f32)
                .astype(bf16)
                .reshape(length, HEADS, HEAD)
            )

        queries, keys, values = project(wq_all), project(wk_all), project(wv_all)
        scores = jnp.einsum("qhd,khd->hqk", queries, keys, preferred_element_type=f32) + bias
        peak = jnp.max(scores, axis=-1, keepdims=True)
        total = jnp.log(jnp.sum(jnp.exp(scores - peak), axis=-1, keepdims=True)) + peak
        probs_b = jnp.exp(scores - total).astype(bf16)
        mixed = (
            jnp.einsum("hqk,khd->qhd", probs_b, values, preferred_element_type=f32)
            .astype(bf16)
            .reshape(length, width)
        )
        resid = acts32 + jnp.dot(mixed, wo_all, preferred_element_type=f32)
        normed_two, scale_two = norm_forward(resid, gain_two32)
        normed_two_b = normed_two.astype(bf16)
        logits = jnp.dot(normed_two_b, wr_all, preferred_element_type=f32) + bias_all32
        router_probs = jax.nn.softmax(logits, axis=-1)
        return dict(
            acts32=acts32, scale_one=scale_one, normed_b=normed_b, queries=queries, keys=keys,
            values=values, probs_b=probs_b, mixed=mixed, resid=resid, scale_two=scale_two,
            normed_two_b=normed_two_b, router_probs=router_probs,
        )

    own = lax.axis_index(AXES) * local_experts

    def expert(rows, raw, local):
        logits = jnp.dot(rows, wr_all, preferred_element_type=f32) + bias_all32
        probs = jax.nn.softmax(logits, axis=-1)
        gate = jnp.sum(jnp.where(expert_ids[None, :] == own + local, probs, 0.0), axis=-1)
        grad_result = (gate[:, None] * raw.astype(f32)).astype(bf16)
        inner = jnp.dot(rows, w_in[local], preferred_element_type=f32)
        active = smooth_unit(inner).astype(bf16)
        result = jnp.dot(active, w_out[local], preferred_element_type=f32).astype(bf16)
        grad_active = jnp.einsum("rd,fd->rf", grad_result, w_out[local], preferred_element_type=f32)
        unused, smooth_pull = jax.vjp(smooth_unit, inner)
        grad_inner = smooth_pull(grad_active)[0].astype(bf16)
        grad_rows = jnp.einsum(
            "rf,df->rd", grad_inner, w_in[local], preferred_element_type=f32
        ).astype(bf16)
        return result, grad_rows, (rows, grad_result, active, grad_inner)

    def back(at, kept, hot, sender, result, grad_back):
        expert_rows = jnp.einsum("ct,cd->td", sender, result, preferred_element_type=f32)
        resid, scale_two = kept["resid"], kept["scale_two"]
        router_probs, normed_two_b = kept["router_probs"], kept["normed_two_b"]
        gate = jnp.sum(router_probs * hot, axis=-1)
        output = (resid + gate[:, None] * expert_rows).astype(bf16)
        upstream32 = upstream_grad[at].astype(f32)
        grad_gate = jnp.sum(upstream32 * expert_rows, axis=-1)
        grad_from_experts = jnp.einsum("ct,cd->td", sender, grad_back, preferred_element_type=f32)
        grad_logits = (
            router_probs * (hot * grad_gate[:, None] - (gate * grad_gate)[:, None])
        ).astype(bf16)
        grad_router_bias = jnp.sum(grad_logits.astype(f32), axis=0)
        grad_router_w = jnp.einsum(
            "td,te->de", normed_two_b, grad_logits, preferred_element_type=f32
        )
        grad_normed_two = (
            jnp.einsum("te,de->td", grad_logits, wr_all, preferred_element_type=f32)
            + grad_from_experts
        )
        grad_resid_norm, grad_gain_two = norm_backward(
            resid, scale_two, gain_two32, grad_normed_two
        )
        grad_resid = upstream32 + grad_resid_norm
        grad_branch = grad_resid.astype(bf16)
        grad_output_w = jnp.einsum(
            "td,te->de", kept["mixed"], grad_branch, preferred_element_type=f32
        )
        grad_mixed = (
            jnp.einsum("te,de->td", grad_branch, wo_all, preferred_element_type=f32)
            .astype(bf16)
            .reshape(length, HEADS, HEAD)
        )
        probs_b = kept["probs_b"]
        probs = probs_b.astype(f32)
        queries, keys, values = kept["queries"], kept["keys"], kept["values"]
        grad_probs = jnp.einsum("qhd,khd->hqk", grad_mixed, values, preferred_element_type=f32)
        center = jnp.sum(probs * grad_probs, axis=-1, keepdims=True)
        grad_scores = (probs * (grad_probs - center)).astype(bf16)
        grad_values = (
            jnp.einsum("hqk,qhd->khd", probs_b, grad_mixed, preferred_element_type=f32)
            .astype(bf16)
            .reshape(length, width)
        )
        grad_queries = (
            jnp.einsum("hqk,khd->qhd", grad_scores, keys, preferred_element_type=f32)
            .astype(bf16)
            .reshape(length, width)
        )
        grad_keys = (
            jnp.einsum("hqk,qhd->khd", grad_scores, queries, preferred_element_type=f32)
            .astype(bf16)
            .reshape(length, width)
        )
        normed_b = kept["normed_b"]
        grad_weights = [
            jnp.einsum("td,te->de", normed_b, grad, preferred_element_type=f32)
            for grad in (grad_queries, grad_keys, grad_values)
        ]
        grad_normed = sum(
            jnp.einsum("te,de->td", grad, weight, preferred_element_type=f32)
            for grad, weight in (
                (grad_queries, wq_all),
                (grad_keys, wk_all),
                (grad_values, wv_all),
            )
        )
        grad_acts_norm, grad_gain_one = norm_backward(
            kept["acts32"], kept["scale_one"], gain_one32, grad_normed
        )
        grad_acts = (grad_resid + grad_acts_norm).astype(bf16)
        fold = jnp.zeros((HEADS, block, span), f32)
        for step in range(blocks):
            low = length - block * (step + 1)
            piece = grad_scores[:, block * step : block * (step + 1), :].astype(f32)
            fold = fold + jnp.pad(piece, ((0, 0), (0, 0), (low, span - length - low)))
        return (
            output,
            grad_acts,
            fold,
            (
                *grad_weights,
                grad_output_w,
                grad_router_w,
                grad_gain_one,
                grad_gain_two,
                grad_router_bias,
            ),
        )

    plans = [plan(at) for at in range(batches)]
    raw_arrived = [dispatch(plans[at][1], upstream_grad[at]) for at in range(batches)]
    fronts, returned, saved = [], [], []
    for at in range(batches):
        kept = front(at)
        fronts.append(kept)
        arrived = dispatch(plans[at][1], kept["normed_two_b"])
        arrived = arrived.reshape(devices, local_experts, capacity, width)
        raw = raw_arrived[at].reshape(devices, local_experts, capacity, width)
        results, grads, keep = [], [], []
        for local in range(local_experts):
            result, grad_rows, held = expert(
                arrived[:, local].reshape(devices * capacity, width),
                raw[:, local].reshape(devices * capacity, width),
                local,
            )
            results.append(result.reshape(devices, capacity, width))
            grads.append(grad_rows.reshape(devices, capacity, width))
            keep.append(held)
        saved.append(keep)
        both = jnp.concatenate(
            [
                jnp.stack(results, axis=1).reshape(devices, local_experts * capacity, width),
                jnp.stack(grads, axis=1).reshape(devices, local_experts * capacity, width),
            ],
            axis=2,
        )
        returned.append(exchange(both).reshape(slots, 2 * width))

    grad_in, grad_out = [], []
    for local in range(local_experts):
        rows, grad_result, active, grad_inner = (
            jnp.concatenate([saved[at][local][i] for at in range(batches)], axis=0)
            for i in range(4)
        )
        grad_in.append(jnp.einsum("rd,rf->df", rows, grad_inner, preferred_element_type=f32))
        grad_out.append(jnp.einsum("rf,rd->fd", active, grad_result, preferred_element_type=f32))

    outputs, grad_inputs, total, folded = [], [], None, None
    for at in range(batches):
        output, grad_acts, fold, update = back(
            at,
            fronts[at],
            plans[at][0],
            plans[at][1],
            returned[at][:, :width],
            returned[at][:, width:],
        )
        outputs.append(output)
        grad_inputs.append(grad_acts)
        folded = fold if folded is None else folded + fold
        total = update if total is None else tuple(a + b for a, b in zip(total, update))
    rows = block
    while rows > 1:
        rows //= 2
        folded = folded[:, :rows] + jnp.roll(folded[:, rows:], -rows, axis=2)
    diagonal = jnp.roll(folded[:, 0], block - 1, axis=1)
    grad_rel = jnp.einsum(
        "hn,bn->bh", diagonal, bucket_hot.astype(f32), precision=lax.Precision.HIGHEST
    ).reshape(-1)
    g_query, g_key, g_value, g_output, g_router, g_gain_one, g_gain_two, g_bias = total

    small_grads = [g_router, g_gain_one, g_gain_two, grad_rel, g_bias]
    small_pack = pack_rows([part.reshape(devices, -1) for part in small_grads], width)
    packed = jnp.concatenate(
        [part.reshape(devices, shard, width) for part in (g_query, g_key, g_value, g_output)]
        + [small_pack],
        axis=1,
    ).astype(bf16)
    depth = packed.shape[1]
    summed = lax.psum_scatter(
        packed.reshape(narrow, wide, depth, width), "wide", scatter_dimension=1, tiled=True
    )
    summed = lax.psum_scatter(
        summed.reshape(narrow, depth, width), "narrow", scatter_dimension=0, tiled=True
    )
    summed = summed.reshape(depth, width).astype(f32)
    r_query, r_key, r_value, r_output = (
        summed[i * shard : (i + 1) * shard] for i in range(4)
    )
    tail = unpack_rows(summed[None, 4 * shard :], [part.size // devices for part in small_grads])
    r_router, r_gain_one, r_gain_two, r_rel, r_bias = (
        part.reshape(shape)
        for part, shape in zip(
            tail,
            (w_router.shape, gain_attn.shape, gain_ffn.shape, rel_bias.shape, router_bias.shape),
        )
    )
    return (
        jnp.stack(outputs, axis=0),
        jnp.stack(grad_inputs, axis=0),
        r_query,
        r_key,
        r_value,
        r_output,
        r_router,
        r_gain_one,
        r_gain_two,
        r_rel,
        r_bias,
        jnp.stack(grad_in, axis=0),
        jnp.stack(grad_out, axis=0),
    )


def solution(mesh):
    both = P(AXES)
    in_specs = (both,) * 14 + (P(), both)
    out_specs = (both,) * 13
    return jax.shard_map(body, mesh=mesh, in_specs=in_specs, out_specs=out_specs, check_vma=False)
```

time: 2930 us -> 644 us (0.22)
  local copies, waits for them, and re-layouts: 1190 us -> 96.7 us
  waiting for transfers between devices: 1000 us -> 206 us
  blocking collectives: 309 us -> 0 us
  matrix products: 317 us -> 229 us
    gather x1 -> x0, local copies, waits for them, and re-layouts: 1040 us -> none  [body(): bucket_map[distance].reshape(1, -1)]
    reduce_scatter x8 -> x2, waiting for transfers between devices: 645 us -> 43.9 us  [the longest x1 35.8 us: body(): lax.psum_scatter(packed.reshape(narrow, wide, depth, width), 'wide', scat...]
    all_gather x8 -> x1, waiting for transfers between devices: 304 us -> 62.7 us  [body(): everything = lax.all_gather(square, AXES, axis=0)]
    while x4 -> x0, blocking collectives: 158 us -> none
    all_gather x2 -> x0, blocking collectives: 110 us -> none  [one_batch(): lax.all_gather(w_router, ('narrow', 'wide'), axis=0, tiled=True)]
    dot_general x67 -> x66, matrix products: 317 us -> 229 us  [the longest x2 45.7 us: expert(): inner = jnp.dot(rows, w_in[local], preferred_element_type=f32)]
    while x186 -> x0, local copies, waits for them, and re-layouts: 67.6 us -> none
    all_to_all x8 -> x6, waiting for transfers between devices: 50.2 us -> 99.5 us  [exchange(): return lax.all_to_all(buffer, AXES, split_axis=0, concat_axis=0, tiled=True)]
  transfers between devices with their start and end apart: 26 -> 9, of which waited for: 20 -> 8; matrix products, arithmetic and copies ran while one was open for 15% -> 25% of each run, Pallas kernels for 0% -> 0%
where the time goes in v1:
time: 644 us; the launch traced here: 634 us
  matrix products  229 us (36%)
  waiting for transfers between devices  206 us (32%)
  local copies, waits for them, and re-layouts  96.7 us (15%)
  other arithmetic  54.7 us (8%)
  starting transfers between devices  25.8 us (4%)
  between operations  16.6 us (3%)
    all_to_all x6, waiting for transfers between devices, exchange(): return lax.all_to_all(buffer, AXES, split_axis=0, concat_axis=0, tiled=True)  99.5 us
    all_gather x1, waiting for transfers between devices, body(): everything = lax.all_gather(square, AXES, axis=0)  62.7 us
    dot_general x2, matrix products, expert(): inner = jnp.dot(rows, w_in[local], preferred_element_type=f32)  45.7 us
    reduce_scatter x1, waiting for transfers between devices, body(): lax.psum_scatter(packed.reshape(narrow, wide, depth, width), 'wide', scat...  35.8 us
    all_to_all x6, starting transfers between devices, exchange(): return lax.all_to_all(buffer, AXES, split_axis=0, concat_axis=0, tiled=True)  25.7 us
    unnamed x289, local copies, waits for them, and re-layouts  23.9 us
    dot_general x2, matrix products, expert(): jnp.einsum('rd,fd->rf', grad_result, w_out[local], preferred_element_type...  19.5 us
    dot_general x2, matrix products, front(): jnp.einsum('qhd,khd->hqk', queries, keys, preferred_element_type=f32) + bias  17.2 us
  transfers between devices with their start and end apart: 9, of which 8 were waited for; matrix products, arithmetic and copies ran while one was open for 25% of the time, Pallas kernels for 0%

profile of v1, /device:TPU:0, one launch (start us, length us, event | category | flops | bytes accessed | tf_op | source)
XLA Modules:
  0.0 634.5 jit_solution(10678120418856835535)
XLA Ops:
  18.2 62.7 %all-gather.4.cloned.1.call-done = bf16[32,98,768]{2,1,0:T(8,128)(2,1)} async-done(((bf16[1,98,768]{2,1,0:T(8,128)(2,1)}), bf16[32,98,768]{2,1,0:T(8,128)(2,1)}) %all-gather.4.cloned.1.call-update) | async-done | bytes 4816912 | tf_op jit(solution)/shard_map/all_gather | solution.py:106
  111.4 10.6 %fusion.177 = (f32[12,128,512]{2,1,0:T(8,128)}, f32[12,128,512]{2,1,0:T(8,128)}, f32[12,128,512]{2,1,0:T(8,128)}, f32[12,128,512]{2,1,0:T(8,128)}) fusion(f32[12,128,1024]{2,1,0:T(8,128)} %shard_map.255), kind=kLoop, calls=%fused_computation.314 | loop fusion | bytes 25165824 | tf_op jit(solution)/shard_map/slice | solution.py:127
  122.0 8.7 %fusion.182 = (f32[12,512]{1,0:T(8,128)S(1)}, f32[12,512,512]{2,1,0:T(8,128)}) fusion(f32[12,128,512]{2,1,0:T(8,128)} %get-tuple-element.46, f32[12,128,512]{2,1,0:T(8,128)} %get-tuple-element.47, f32[12,128,512]{2,1,0:T(8,128)} %get-tuple-element.48, f32[12,128,512]{2,1,0:T(8,128)} %get-tuple-element.45, bf16[512,12,64]{0,2,1:T(8,128)(2,1)S(1)} %bitcast.316, ...), kind=kOutput, calls=%fused_computation.319 | convolution fusion | flops 418375680 | bytes 26763264 | tf_op jit(solution)/shard_map/qhd,khd->hqk/dot_general | solution.py:161
  130.7 6.4 %exponential_reduce_fusion = f32[12,512]{1,0:T(8,128)S(1)} fusion(f32[12,512,512]{2,1,0:T(8,128)} %get-tuple-element.88, f32[12,512]{1,0:T(8,128)S(1)} %get-tuple-element.87), kind=kLoop, calls=%fused_computation.10 | loop fusion | flops 6285312 | bytes 12632064 | tf_op jit(solution)/shard_map/reduce_sum | solution.py:163
  137.2 8.5 %fusion.181 = (f32[12,512]{1,0:T(8,128)S(1)}, f32[12,512,512]{2,1,0:T(8,128)}) fusion(f32[12,128,512]{2,1,0:T(8,128)} %get-tuple-element.46, f32[12,128,512]{2,1,0:T(8,128)} %get-tuple-element.47, f32[12,128,512]{2,1,0:T(8,128)} %get-tuple-element.48, f32[12,128,512]{2,1,0:T(8,128)} %get-tuple-element.45, bf16[512,12,64]{0,2,1:T(8,128)(2,1)S(1)} %bitcast.314, ...), kind=kOutput, calls=%fused_computation.318 | convolution fusion | flops 418375680 | bytes 26763264 | tf_op jit(solution)/shard_map/qhd,khd->hqk/dot_general | solution.py:161
  145.7 7.6 %exponential_reduce_fusion.1 = f32[12,512]{1,0:T(8,128)S(1)} fusion(f32[12,512,512]{2,1,0:T(8,128)} %get-tuple-element.84, f32[12,512]{1,0:T(8,128)S(1)} %get-tuple-element.83), kind=kLoop, calls=%fused_computation.12 | loop fusion | flops 6285312 | bytes 12632064 | tf_op jit(solution)/shard_map/reduce_sum | solution.py:163
  186.7 17.3 %all-to-all-done.3 = bf16[32,20,768]{2,1,0:T(8,128)(2,1)S(1)} async-done(((bf16[32,20,768]{2,1,0:T(8,128)(2,1)}), bf16[32,20,768]{2,1,0:T(8,128)(2,1)S(1)}, u32[]{:S(2)}, u32[]{:S(2)}) %all-to-all-start.3) | async-done | bytes 983072 | tf_op jit(solution)/shard_map/all_to_all | solution.py:36
  208.0 22.8 %multiply_convert_fusion = (bf16[640,3072]{1,0:T(8,128)(2,1)}, f32[640,3072]{1,0:T(8,128)}, f32[640,3072]{1,0:T(8,128)}) fusion(bf16[640,768]{1,0:T(8,128)(2,1)S(1)} %reshape_squeeze_reshape.9, bf16[1,768,3072]{2,1,0:T(8,128)(2,1)} %param.26), kind=kOutput, calls=%fused_computation.26 | convolution fusion | flops 3147694080 | bytes 25362432 | tf_op jit(solution)/shard_map/dot_general | solution.py:188
  242.3 22.8 %multiply_convert_fusion.1 = (bf16[640,3072]{1,0:T(8,128)(2,1)}, f32[640,3072]{1,0:T(8,128)}, f32[640,3072]{1,0:T(8,128)}) fusion(bf16[640,768]{1,0:T(8,128)(2,1)S(1)} %reshape_squeeze_reshape.8, bf16[1,768,3072]{2,1,0:T(8,128)(2,1)} %param.26), kind=kOutput, calls=%fused_computation.40 | convolution fusion | flops 3147694080 | bytes 25362432 | tf_op jit(solution)/shard_map/dot_general | solution.py:188
  276.5 9.7 %add_convert_fusion = bf16[640,3072]{1,0:T(8,128)(2,1)S(1)} fusion(f32[640,3072]{1,0:T(8,128)} %get-tuple-element.36, f32[640,3072]{1,0:T(8,128)} %get-tuple-element.98, bf16[640,768]{1,0:T(8,128)(2,1)S(1)} %convert_element_type.396, bf16[1,3072,768]{2,1,0:T(8,128)(2,1)} %param.27), kind=kOutput, calls=%fused_computation.25 | convolution fusion | flops 3047424000 | bytes 25362432 | tf_op jit(solution)/shard_map/rd,fd->rf/dot_general | solution.py:191
  294.0 6.7 %fusion.99 = bf16[640,768]{1,0:T(8,128)(2,1)S(1)} fusion(bf16[640,3072]{1,0:T(8,128)(2,1)} %get-tuple-element.35, bf16[1,3072,768]{2,1,0:T(8,128)(2,1)} %param.27), kind=kOutput, calls=%fused_computation.153 | convolution fusion | flops 3020390400 | bytes 9633792 | tf_op jit(solution)/shard_map/dot_general | solution.py:190
  304.7 6.3 all-to-all-start.5
  311.5 9.7 %add_convert_fusion.1 = bf16[640,3072]{1,0:T(8,128)(2,1)S(1)} fusion(f32[640,3072]{1,0:T(8,128)} %get-tuple-element.34, f32[640,3072]{1,0:T(8,128)} %get-tuple-element.93, bf16[640,768]{1,0:T(8,128)(2,1)S(1)} %convert_element_type.371, bf16[1,3072,768]{2,1,0:T(8,128)(2,1)} %param.27), kind=kOutput, calls=%fused_computation.39 | convolution fusion | flops 3047424000 | bytes 25362432 | tf_op jit(solution)/shard_map/rd,fd->rf/dot_general | solution.py:191
  329.1 6.7 %fusion.96 = bf16[640,768]{1,0:T(8,128)(2,1)S(1)} fusion(bf16[640,3072]{1,0:T(8,128)(2,1)} %get-tuple-element.33, bf16[1,3072,768]{2,1,0:T(8,128)(2,1)} %param.27), kind=kOutput, calls=%fused_computation.152 | convolution fusion | flops 3020390400 | bytes 9633792 | tf_op jit(solution)/shard_map/dot_general | solution.py:190
  337.7 27.8 %all-to-all-done.5 = bf16[32,20,1536]{2,1,0:T(8,128)(2,1)} async-done(((bf16[32,20,1536]{2,1,0:T(8,128)(2,1)}), bf16[32,20,1536]{2,1,0:T(8,128)(2,1)}, u32[]{:S(2)}, u32[]{:S(2)}) %all-to-all-start.5) | async-done | bytes 1966112 | tf_op jit(solution)/shard_map/all_to_all | solution.py:36
  379.2 44.8 %all-to-all-done.2 = bf16[32,20,1536]{2,1,0:T(8,128)(2,1)S(1)} async-done(((bf16[32,20,1536]{2,1,0:T(8,128)(2,1)}), bf16[32,20,1536]{2,1,0:T(8,128)(2,1)S(1)}, u32[]{:S(2)}, u32[]{:S(2)}) %all-to-all-start.2) | async-done | bytes 1966112 | tf_op jit(solution)/shard_map/all_to_all | solution.py:36
  450.4 6.6 %fusion.2 = (f32[12,512]{1,0:T(8,128)S(1)}, f32[12,512,512]{2,1,0:T(8,128)}) fusion(bf16[12,512,512]{2,1,0:T(8,128)(2,1)S(1)} %bitcast.297, bf16[512,12,64]{0,2,1:T(8,128)(2,1)S(1)} %bitcast.305, bf16[512,12,64]{0,2,1:T(8,128)(2,1)S(1)} %bitcast.313), kind=kOutput, calls=%fused_computation.6 | convolution fusion | flops 412084224 | bytes 20471808 | tf_op jit(solution)/shard_map/qhd,khd->hqk/dot_general | solution.py:235
  457.0 6.5 %fusion.3 = bf16[12,512,512]{2,1,0:T(8,128)(2,1)S(1)} fusion(f32[12,512,512]{2,1,0:T(8,128)} %get-tuple-element.106, f32[12,512]{1,0:T(8,128)S(1)} %get-tuple-element.105, f32[12,512,512]{2,1,0:T(8,128)S(1)} %bitcast.303, f32[12,512]{1,0:T(8,128)S(1)} %copy-done.74), kind=kLoop, calls=%fused_computation.7 | loop fusion | flops 18874368 | bytes 31506432 | tf_op jit(solution)/shard_map/convert_element_type | solution.py:237
  477.8 6.6 %fusion = (f32[12,512]{1,0:T(8,128)S(1)}, f32[12,512,512]{2,1,0:T(8,128)}) fusion(bf16[12,512,512]{2,1,0:T(8,128)(2,1)S(1)} %bitcast.295, bf16[512,12,64]{0,2,1:T(8,128)(2,1)S(1)} %bitcast.307, bf16[512,12,64]{0,2,1:T(8,128)(2,1)S(1)} %bitcast.311), kind=kOutput, calls=%fused_computation.4 | convolution fusion | flops 412084224 | bytes 20471808 | tf_op jit(solution)/shard_map/qhd,khd->hqk/dot_general | solution.py:235
  484.4 6.4 %fusion.1 = bf16[12,512,512]{2,1,0:T(8,128)(2,1)S(1)} fusion(f32[12,512,512]{2,1,0:T(8,128)} %get-tuple-element.104, f32[12,512]{1,0:T(8,128)S(1)} %get-tuple-element.103, f32[12,512,512]{2,1,0:T(8,128)S(1)} %bitcast.299, f32[12,512]{1,0:T(8,128)S(1)} %copy-done.72), kind=kLoop, calls=%fused_computation.5 | loop fusion | flops 18874368 | bytes 31506432 | tf_op jit(solution)/shard_map/convert_element_type | solution.py:237
  552.4 10.7 %fusion.29 = f32[1,3072,768]{2,1,0:T(8,128)} fusion(bf16[640,3072]{1,0:T(8,128)(2,1)S(1)} %copy-done.124, bf16[640,3072]{1,0:T(8,128)(2,1)} %get-tuple-element.33, bf16[640,768]{1,0:T(8,128)(2,1)S(1)} %multiply_convert_fusion.4, bf16[640,768]{1,0:T(8,128)(2,1)S(1)} %multiply_convert_fusion.5), kind=kOutput, calls=%fused_computation.59 | convolution fusion | flops 6059458560 | bytes 19267584 | tf_op jit(solution)/shard_map/rf,rd->fd/dot_general | solution.py:325
  563.1 35.8 %reduce-scatter.3.cloned.1.call-done = bf16[4,1,98,768]{3,2,0,1:T(8,128)(2,1)} async-done(((bf16[4,8,98,768]{3,2,0,1:T(8,128)(2,1)}), bf16[4,1,98,768]{3,2,0,1:T(8,128)(2,1)}) %reduce-scatter.3.cloned.1.call-update) | async-done | bytes 602128 | tf_op jit(solution)/shard_map/reduce_scatter | solution.py:359
  598.9 11.6 %fusion.26 = f32[1,768,3072]{2,1,0:T(8,128)} fusion(bf16[640,3072]{1,0:T(8,128)(2,1)} %copy-done.122, bf16[640,3072]{1,0:T(8,128)(2,1)} %copy-done.123, bf16[640,768]{1,0:T(8,128)(2,1)} %copy-done.45, bf16[640,768]{1,0:T(8,128)(2,1)} %copy-done.46), kind=kOutput, calls=%fused_computation.58 | convolution fusion | flops 6059458560 | bytes 19267584 | tf_op jit(solution)/shard_map/rd,rf->df/dot_general | solution.py:324
  615.3 8.2 %reduce-scatter.5.cloned.1.call-done = bf16[1,98,768]{2,1,0:T(8,128)(2,1)} async-done(((bf16[4,98,768]{2,1,0:T(8,128)(2,1)}), bf16[1,98,768]{2,1,0:T(8,128)(2,1)}) %reduce-scatter.5.cloned.1.call-update) | async-done | bytes 150544 | tf_op jit(solution)/shard_map/reduce_scatter | solution.py:362
  (489 shorter events, 246.1 us)
Async XLA Ops:
  7.2 73.8 %all-gather.4.cloned.1.call-start = ((), (), s32[]{:S(2)}) async-start(), calls=%async_computation.10 | async-start | bytes 5271552 | tf_op jit(solution)/shard_map/all_gather | solution.py:106
  14.0 81.1 %copy-start.103 = (s32[1024]{0:T(1024)}, s32[1024]{0:T(1024)S(1)}, u32[]{:S(2)}) copy-start(s32[1024]{0:T(1024)S(1)} %pad.66) | copy-start | bytes 12292
  14.7 164.4 %copy-start.97 = (s32[1,512,1]{1,2,0:T(1,128)}, s32[1,512,1]{1,2,0:T(1,128)S(1)}, u32[]{:S(2)}) copy-start(s32[1,512,1]{1,2,0:T(1,128)S(1)} %get-tuple-element.71) | copy-start | bytes 6148
  17.6 157.3 %copy-start.105 = (s32[512]{0:T(512)}, s32[512]{0:T(512)S(1)}, u32[]{:S(2)}) copy-start(s32[512]{0:T(512)S(1)} %add_select_fusion) | copy-start | bytes 6148
  18.2 73.3 %copy-start.82 = (f32[512]{0:T(512)}, f32[512]{0:T(512)S(1)}, u32[]{:S(2)}) copy-start(f32[512]{0:T(512)S(1)} %get-tuple-element.78) | copy-start | bytes 6148
  18.2 75.0 %copy-start.84 = (f32[512]{0:T(512)}, f32[512]{0:T(512)S(1)}, u32[]{:S(2)}) copy-start(f32[512]{0:T(512)S(1)} %get-tuple-element.108) | copy-start | bytes 6148
  95.1 72.8 %copy-start.80 = (f32[768]{0:T(1024)}, f32[768]{0:T(1024)S(1)}, u32[]{:S(2)}) copy-start(f32[768]{0:T(1024)S(1)} %reshape.602) | copy-start | bytes 9220
  100.9 62.7 %copy-start.24 = (bf16[512,768]{0,1:T(8,128)(2,1)}, bf16[512,768]{0,1:T(8,128)(2,1)S(1)}, u32[]{:S(2)}) copy-start(bf16[512,768]{0,1:T(8,128)(2,1)S(1)} %copy.73) | copy-start | bytes 2359300
  106.1 49.9 %copy-start.22 = (bf16[512,768]{0,1:T(8,128)(2,1)}, bf16[512,768]{0,1:T(8,128)(2,1)S(1)}, u32[]{:S(2)}) copy-start(bf16[512,768]{0,1:T(8,128)(2,1)S(1)} %copy.69) | copy-start | bytes 2359300
  171.2 32.8 %all-to-all-start.3 = ((bf16[32,20,768]{2,1,0:T(8,128)(2,1)}), bf16[32,20,768]{2,1,0:T(8,128)(2,1)S(1)}, u32[]{:S(2)}, u32[]{:S(2)}) async-start(bf16[32,20,768]{2,1,0:T(8,128)(2,1)} %reshape.582), calls=%async_computation.3 | async-start | bytes 2359296 | tf_op jit(solution)/shard_map/all_to_all | solution.py:36
  186.7 78.9 %copy-start.108 = (f32[32]{0:T(128)}, f32[32]{0:T(128)S(1)}, u32[]{:S(2)}) copy-start(f32[32]{0:T(128)S(1)} %bitcast_convert_fusion) | copy-start | bytes 388
  204.0 32.9 %all-to-all-start = ((bf16[32,20,768]{2,1,0:T(8,128)(2,1)}), bf16[32,20,768]{2,1,0:T(8,128)(2,1)}, u32[]{:S(2)}, u32[]{:S(2)}) async-start(bf16[32,20,768]{2,1,0:T(8,128)(2,1)} %reshape.575), calls=%async_computation | async-start | bytes 2359296 | tf_op jit(solution)/shard_map/all_to_all | solution.py:36
  208.0 57.6 %copy-start.45 = (bf16[640,768]{1,0:T(8,128)(2,1)}, bf16[640,768]{1,0:T(8,128)(2,1)S(1)}, u32[]{:S(2)}) copy-start(bf16[640,768]{1,0:T(8,128)(2,1)S(1)} %reshape_squeeze_reshape.9) | copy-start | bytes 2949124
  236.8 33.2 %all-to-all-start.4 = ((bf16[32,20,768]{2,1,0:T(8,128)(2,1)}), bf16[32,20,768]{2,1,0:T(8,128)(2,1)S(1)}, u32[]{:S(2)}, u32[]{:S(2)}) async-start(bf16[32,20,768]{2,1,0:T(8,128)(2,1)} %reshape.583), calls=%async_computation.4 | async-start | bytes 2359296 | tf_op jit(solution)/shard_map/all_to_all | solution.py:36
  270.0 34.7 %all-to-all-start.1 = ((bf16[32,20,768]{2,1,0:T(8,128)(2,1)}), bf16[32,20,768]{2,1,0:T(8,128)(2,1)S(1)}, u32[]{:S(2)}, u32[]{:S(2)}) async-start(bf16[32,20,768]{2,1,0:T(8,128)(2,1)} %reshape.576), calls=%async_computation.1 | async-start | bytes 2359296 | tf_op jit(solution)/shard_map/all_to_all | solution.py:36
  304.7 60.8 %all-to-all-start.5 = ((bf16[32,20,1536]{2,1,0:T(8,128)(2,1)}), bf16[32,20,1536]{2,1,0:T(8,128)(2,1)}, u32[]{:S(2)}, u32[]{:S(2)}) async-start(bf16[32,20,1536]{2,1,0:T(8,128)(2,1)} %pad_maximum_fusion.2), calls=%async_computation.5 | async-start | bytes 4718592 | tf_op jit(solution)/shard_map/all_to_all | solution.py:36
  337.7 31.9 %copy-start.27 = (bf16[512,768]{1,0:T(8,128)(2,1)S(1)}, bf16[512,768]{1,0:T(8,128)(2,1)}, u32[]{:S(2)}) copy-start(bf16[512,768]{1,0:T(8,128)(2,1)} %copy-done.26) | copy-start | bytes 2359300
  337.7 31.9 %copy-start.109 = (f32[32]{0:T(128)S(1)}, f32[32]{0:T(128)}, u32[]{:S(2)}) copy-start(f32[32]{0:T(128)} %copy-done.108) | copy-start | bytes 388
  337.7 33.9 %copy-start.98 = (s32[1,512,1]{1,2,0:T(1,128)S(1)}, s32[1,512,1]{1,2,0:T(1,128)}, u32[]{:S(2)}) copy-start(s32[1,512,1]{1,2,0:T(1,128)} %copy-done.97) | copy-start | bytes 6148
  337.7 33.9 %copy-start.96 = (s32[1,512,1]{1,2,0:T(1,128)S(1)}, s32[1,512,1]{1,2,0:T(1,128)}, u32[]{:S(2)}) copy-start(s32[1,512,1]{1,2,0:T(1,128)} %copy-done.95) | copy-start | bytes 6148
  365.5 58.5 %all-to-all-start.2 = ((bf16[32,20,1536]{2,1,0:T(8,128)(2,1)}), bf16[32,20,1536]{2,1,0:T(8,128)(2,1)S(1)}, u32[]{:S(2)}, u32[]{:S(2)}) async-start(bf16[32,20,1536]{2,1,0:T(8,128)(2,1)} %pad_maximum_fusion.1), calls=%async_computation.2 | async-start | bytes 4718592 | tf_op jit(solution)/shard_map/all_to_all | solution.py:36
  369.5 229.3 %reduce-scatter.3.cloned.1.call-start = ((), (), s32[]{:S(2)}) async-start(), calls=%async_computation.8 | async-start | bytes 5750784 | tf_op jit(solution)/shard_map/reduce_scatter | solution.py:359
  379.2 46.8 %copy-start.113 = (s32[512]{0:T(512)S(1)}, s32[512]{0:T(512)}, u32[]{:S(2)}) copy-start(s32[512]{0:T(512)} %copy-done.112) | copy-start | bytes 6148
  543.5 79.9 %reduce-scatter.5.cloned.1.call-start = ((), (), s32[]{:S(2)}) async-start(), calls=%async_computation.9 | async-start | bytes 798720 | tf_op jit(solution)/shard_map/reduce_scatter | solution.py:362
  (123 other events, 573.4 us)
Sparse Core Ops, SparseCore 0:
  13.4 67.5 all-gather.3
  543.6 55.1 reduce-scatter.2
  601.1 22.2 reduce-scatter.4

commit v2 on v1

v2 whole, which is shorter than its diff:
```python
import jax
import jax.numpy as jnp
from jax import lax
from jax.experimental import pallas as pl
from jax.experimental.pallas import tpu as pltpu
from jax.sharding import PartitionSpec as P

HEADS = 12
HEAD = 64
BUCKETS = 32
PAIR = 2 * HEAD
GROUP = 4
BLOCK = 128
AXES = ("narrow", "wide")
VMEM_BYTES = 60 * 1024 * 1024

epsilon = 1e-06
f32 = jnp.float32
bf16 = jnp.bfloat16


def mm(a, b):
    return lax.dot_general(a, b, (((1,), (0,)), ((), ())), preferred_element_type=f32)


def mm_nt(a, b):
    return lax.dot_general(a, b, (((1,), (1,)), ((), ())), preferred_element_type=f32)


def mm_tn(a, b):
    return lax.dot_general(a, b, (((0,), (0,)), ((), ())), preferred_element_type=f32)


def norm_scale(values):
    return lax.rsqrt(jnp.mean(values * values, axis=-1, keepdims=True) + epsilon)


def softmax_rows(logits):
    shifted = jnp.exp(logits - jnp.max(logits, axis=-1, keepdims=True))
    return shifted / jnp.sum(shifted, axis=-1, keepdims=True)


def pair_mask(shape, half):
    lane = lax.broadcasted_iota(jnp.int32, shape, 1)
    return (lane < HEAD) if half == 0 else (lane >= HEAD)


def params():
    return pltpu.CompilerParams(vmem_limit_bytes=VMEM_BYTES)


def front_kernel(
    tokens_ref, wq_ref, wk_ref, wv_ref, wo_ref, skew_ref, gain_one_ref, gain_two_ref, wr_ref,
    rbias_ref, spots_ref, q_ref, k_ref, v_ref, probs_ref, mixed_ref, resid_ref, normed_two_ref,
    router_ref, sent_ref, normed_ref,
):
    step = pl.program_id(0)
    length, width = tokens_ref.shape

    @pl.when(step == 0)
    def start():
        acts = tokens_ref[...].astype(f32)
        normed_ref[...] = (acts * norm_scale(acts) * gain_one_ref[...]).astype(bf16)
        resid_ref[...] = acts

    normed = normed_ref[...]
    q_ref[...] = mm(normed, wq_ref[...]).astype(bf16)
    k_ref[...] = mm(normed, wk_ref[...]).astype(bf16)
    v_ref[...] = mm(normed, wv_ref[...]).astype(bf16)
    for pair in range(GROUP // 2):
        cols = slice(PAIR * pair, PAIR * (pair + 1))
        query, key, value = q_ref[:, cols], k_ref[:, cols], v_ref[:, cols]
        out = None
        for half in range(2):
            head = 2 * pair + half
            mask = pair_mask(query.shape, half)
            scores = mm_nt(jnp.where(mask, query, jnp.zeros_like(query)), key)
            parts = []
            for at in range(length // BLOCK):
                low = length - BLOCK * (at + 1)
                part = scores[BLOCK * at : BLOCK * (at + 1), :] + skew_ref[head, :, low : low + length]
                part = jnp.exp(part - jnp.max(part, axis=-1, keepdims=True))
                total = jnp.sum(part, axis=-1, keepdims=True)
                parts.append((part * (1.0 / total)).astype(bf16))
            probs = jnp.concatenate(parts, axis=0)
            probs_ref[head] = probs
            term = mm(probs, jnp.where(mask, value, jnp.zeros_like(value)))
            out = term if out is None else out + term
        mixed_ref[:, cols] = out.astype(bf16)
    resid_ref[...] += mm(mixed_ref[...], wo_ref[...])

    @pl.when(step == pl.num_programs(0) - 1)
    def finish():
        resid = resid_ref[...]
        normed_two = (resid * norm_scale(resid) * gain_two_ref[...]).astype(bf16)
        normed_two_ref[...] = normed_two
        router_ref[...] = softmax_rows(mm(normed_two, wr_ref[...]) + rbias_ref[...])
        rows = lax.broadcasted_iota(jnp.int32, (sent_ref.shape[0], length), 0)
        left = mm((rows == spots_ref[0:1, :]).astype(bf16), normed_two[:, : width // 2])
        right = mm((rows == spots_ref[1:2, :]).astype(bf16), normed_two[:, width // 2 :])
        sent_ref[...] = (left + right).astype(bf16)


def front_call(tokens, wq, wk, wv, wo, skewed, gain_one, gain_two, wr, rbias, spots, slots):
    length, width = tokens.shape
    experts = wr.shape[1]
    part = GROUP * HEAD
    whole = lambda *shape: pl.BlockSpec(shape, lambda g: (0,) * len(shape))
    columns = lambda size: pl.BlockSpec((size, part), lambda g: (0, g))
    return pl.pallas_call(
        front_kernel,
        grid=(HEADS // GROUP,),
        in_specs=[
            whole(length, width), columns(width), columns(width), columns(width),
            pl.BlockSpec((part, width), lambda g: (g, 0)),
            pl.BlockSpec((GROUP, BLOCK, 2 * length), lambda g: (g, 0, 0)),
            whole(1, width), whole(1, width), whole(width, experts), whole(1, experts),
            whole(2, length),
        ],
        out_specs=[
            columns(length), columns(length), columns(length),
            pl.BlockSpec((GROUP, length, length), lambda g: (g, 0, 0)),
            columns(length), whole(length, width), whole(length, width), whole(length, experts),
            whole(2 * slots, width // 2),
        ],
        out_shape=[
            jax.ShapeDtypeStruct((length, width), bf16),
            jax.ShapeDtypeStruct((length, width), bf16),
            jax.ShapeDtypeStruct((length, width), bf16),
            jax.ShapeDtypeStruct((HEADS, length, length), bf16),
            jax.ShapeDtypeStruct((length, width), bf16),
            jax.ShapeDtypeStruct((length, width), f32),
            jax.ShapeDtypeStruct((length, width), bf16),
            jax.ShapeDtypeStruct((length, experts), f32),
            jax.ShapeDtypeStruct((2 * slots, width // 2), bf16),
        ],
        scratch_shapes=[pltpu.VMEM((length, width), bf16)],
        compiler_params=params(),
        cost_estimate=pl.CostEstimate(
            flops=2 * length * width * width * 4 + 4 * length * length * width * 4,
            bytes_accessed=25 * 1024 * 1024, transcendentals=HEADS * length * length,
        ),
        name="front",
    )(tokens, wq, wk, wv, wo, skewed, gain_one, gain_two, wr, rbias, spots)


def bell(values):
    size = jnp.abs(values)
    t = 1.0 / (1.0 + (0.3275911 * 0.7071067811865476) * size)
    falling = jnp.exp(-0.5 * values * values)
    poly = t * (
        0.127414796
        + t * (-0.142248368 + t * (0.7107068705 + t * (-0.7265760135 + t * 0.5307027145)))
    )
    tail = poly * falling
    return jnp.where(values < 0, tail, 1.0 - tail), falling * 0.3989422804014327


def expert_kernel(
    own_ref, arrived_ref, raw_ref, wr_ref, rbias_ref, place_ref, placed_ref, win_ref, wout_ref,
    sent_ref, rows_ref, active_ref, gradinner_ref, gradresult_ref, result_acc, rows_acc,
):
    step = pl.program_id(0)
    last = pl.num_programs(0) - 1
    count = rows_ref.shape[0]

    @pl.when(step == 0)
    def start():
        arrived = arrived_ref[...]
        ids = lax.broadcasted_iota(jnp.int32, (count, 2 * count), 1)
        half = arrived.shape[1]
        for side in range(2):
            pick = (ids == place_ref[:, side : side + 1]).astype(bf16)
            rows_ref[:, half * side : half * (side + 1)] = mm(pick, arrived).astype(bf16)
        probs = softmax_rows(mm(rows_ref[...], wr_ref[...]) + rbias_ref[...])
        mine = lax.broadcasted_iota(jnp.int32, probs.shape, 1) == own_ref[0]
        gate = jnp.sum(jnp.where(mine, probs, 0.0), axis=-1, keepdims=True)
        gradresult_ref[...] = (gate * raw_ref[...].astype(f32)).astype(bf16)

    inner = mm(rows_ref[...], win_ref[...])
    grad_active = mm_nt(gradresult_ref[...], wout_ref[...])
    share, density = bell(inner)
    active = (inner * share).astype(bf16)
    grad_inner = (grad_active * (share + inner * density)).astype(bf16)
    active_ref[...] = active
    gradinner_ref[...] = grad_inner
    result = mm(active, wout_ref[...])
    grad_rows = mm_nt(grad_inner, win_ref[...])

    @pl.when(step == 0)
    def first():
        result_acc[...] = result
        rows_acc[...] = grad_rows

    @pl.when(step > 0)
    def more():
        result_acc[...] += result
        rows_acc[...] += grad_rows

    @pl.when(step == last)
    def finish():
        ids = lax.broadcasted_iota(jnp.int32, (2 * count, count), 0)
        sent_ref[...] = (
            mm((ids == placed_ref[0:1, :]).astype(bf16), result_acc[...].astype(bf16))
            + mm((ids == placed_ref[1:2, :]).astype(bf16), rows_acc[...].astype(bf16))
        ).astype(bf16)


def expert_call(own, arrived, raw, wr, rbias, place, w_in, w_out, part=1024):
    count, width = raw.shape
    hidden = w_in.shape[1]
    experts = wr.shape[1]
    whole = lambda *shape: pl.BlockSpec(shape, lambda g, own: (0,) * len(shape))
    columns = lambda n: pl.BlockSpec((n, part), lambda g, own: (0, g))
    return pl.pallas_call(
        expert_kernel,
        grid_spec=pltpu.PrefetchScalarGridSpec(
            num_scalar_prefetch=1,
            grid=(hidden // part,),
            in_specs=[
                whole(2 * count, width // 2), whole(count, width), whole(width, experts),
                whole(1, experts), whole(count, 2), whole(2, count),
                columns(width), pl.BlockSpec((part, width), lambda g, own: (g, 0)),
            ],
            out_specs=[
                whole(2 * count, width), whole(count, width), columns(count), columns(count),
                whole(count, width),
            ],
            scratch_shapes=[pltpu.VMEM((count, width), f32), pltpu.VMEM((count, width), f32)],
        ),
        out_shape=[
            jax.ShapeDtypeStruct((2 * count, width), bf16),
            jax.ShapeDtypeStruct((count, width), bf16),
            jax.ShapeDtypeStruct((count, hidden), bf16),
            jax.ShapeDtypeStruct((count, hidden), bf16),
            jax.ShapeDtypeStruct((count, width), bf16),
        ],
        compiler_params=params(),
        cost_estimate=pl.CostEstimate(
            flops=8 * count * width * hidden, bytes_accessed=20 * 1024 * 1024,
            transcendentals=count * hidden,
        ),
        name="expert",
    )(own, arrived, raw, wr, rbias, place, place.T, w_in, w_out)


def back_kernel(
    target_ref, route_ref, returned_ref, up_ref, resid_ref, router_ref, normed_two_ref,
    mixed_ref, tokens_ref, gain_one_ref, gain_two_ref, wr_ref, wo_ref, wq_ref, wk_ref, wv_ref,
    q_ref, k_ref, v_ref, probs_ref,
    output_ref, gradacts_ref, fold_ref, gq_ref, gk_ref, gv_ref, go_ref, grw_ref, small_ref,
    gbias_ref,
    gradmixed_ref, gradresid_ref, normedt_ref, acc_ref, center_ref,
):
    step = pl.program_id(0)
    last = pl.num_programs(0) - 1
    length, width = tokens_ref.shape
    experts = wr_ref.shape[1]
    part = GROUP * HEAD

    @pl.when(step == 0)
    def start():
        returned = returned_ref[...]
        ids = lax.broadcasted_iota(jnp.int32, (length, returned.shape[0]), 1)
        expert_rows = mm((ids == target_ref[:, 0:1]).astype(bf16), returned)
        grad_back = mm((ids == target_ref[:, 1:2]).astype(bf16), returned)
        up = up_ref[...].astype(f32)
        resid = resid_ref[...]
        router = router_ref[...]
        hot = lax.broadcasted_iota(jnp.int32, (length, experts), 1) == route_ref[...]
        gate = jnp.sum(jnp.where(hot, router, 0.0), axis=-1, keepdims=True)
        output_ref[...] = (resid + gate * expert_rows).astype(bf16)
        grad_gate = jnp.sum(up * expert_rows, axis=-1, keepdims=True)
        grad_logits = (router * (jnp.where(hot, grad_gate, 0.0) - gate * grad_gate)).astype(bf16)
        gbias_ref[...] = jnp.sum(grad_logits.astype(f32), axis=0, keepdims=True)
        grw_ref[...] = mm_tn(normed_two_ref[...], grad_logits)
        grad_normed = mm_nt(grad_logits, wr_ref[...]) + grad_back
        gain = gain_two_ref[...]
        scale = norm_scale(resid)
        small_ref[1:2, :] = jnp.sum(grad_normed * resid * scale, axis=0, keepdims=True)
        weighted = grad_normed * gain
        slope = scale * scale * scale * jnp.mean(weighted * resid, axis=-1, keepdims=True)
        grad_resid = up + (scale * weighted - resid * slope)
        gradresid_ref[...] = grad_resid
        grad_branch = grad_resid.astype(bf16)
        go_ref[...] = mm_tn(mixed_ref[...], grad_branch)
        grad_mixed = mm_nt(grad_branch, wo_ref[...]).astype(bf16)
        products = (grad_mixed.astype(f32) * mixed_ref[...].astype(f32)).astype(f32)
        for g in range(width // part):
            gradmixed_ref[g] = grad_mixed[:, g * part : (g + 1) * part]
            center_ref[g] = products[:, g * part : (g + 1) * part]
        acts = tokens_ref[...].astype(f32)
        normed = (acts * norm_scale(acts) * gain_one_ref[...]).astype(bf16)
        normedt_ref[...] = normed.T

    grad_mixed = gradmixed_ref[step]
    products = center_ref[step]
    dq, dk, dv = [], [], []
    for pair in range(GROUP // 2):
        cols = slice(PAIR * pair, PAIR * (pair + 1))
        query, key, value = q_ref[:, cols], k_ref[:, cols], v_ref[:, cols]
        grad = grad_mixed[:, cols]
        product = products[:, cols]
        gq = gk = gv = None
        for half in range(2):
            head = 2 * pair + half
            mask = pair_mask(query.shape, half)
            clear = lambda a: jnp.where(mask, a, jnp.zeros_like(a))
            own = clear(grad)
            center = jnp.sum(clear(product), axis=-1, keepdims=True)
            probs = probs_ref[head]
            grad_probs = mm_nt(own, value)
            grad_scores = probs.astype(f32) * (grad_probs - center)
            for at in range(length // BLOCK):
                low = length - BLOCK * (at + 1)
                piece = grad_scores[BLOCK * at : BLOCK * (at + 1), :]
                if at == 0:
                    fold_ref[head, :, :low] = jnp.zeros((BLOCK, low), f32)
                    fold_ref[head, :, low : low + length] = piece
                    fold_ref[head, :, low + length :] = jnp.zeros((BLOCK, length - low), f32)
                else:
                    fold_ref[head, :, low : low + length] += piece
            grad_scores = grad_scores.astype(bf16)
            a = mm(grad_scores, clear(key))
            b = mm_tn(grad_scores, clear(query))
            c = mm_tn(probs, own)
            gq = a if gq is None else gq + a
            gk = b if gk is None else gk + b
            gv = c if gv is None else gv + c
        dq.append(gq.astype(bf16))
        dk.append(gk.astype(bf16))
        dv.append(gv.astype(bf16))
    dq, dk, dv = (jnp.concatenate(x, axis=1) for x in (dq, dk, dv))
    normedt = normedt_ref[...]
    gq_ref[...] = mm(normedt, dq)
    gk_ref[...] = mm(normedt, dk)
    gv_ref[...] = mm(normedt, dv)
    total = mm_nt(dq, wq_ref[...]) + mm_nt(dk, wk_ref[...]) + mm_nt(dv, wv_ref[...])

    @pl.when(step == 0)
    def first():
        acc_ref[...] = total

    @pl.when(step > 0)
    def more():
        acc_ref[...] += total

    @pl.when(step == last)
    def finish():
        grad_normed = acc_ref[...]
        acts = tokens_ref[...].astype(f32)
        scale = norm_scale(acts)
        small_ref[0:1, :] = jnp.sum(grad_normed * acts * scale, axis=0, keepdims=True)
        weighted = grad_normed * gain_one_ref[...]
        slope = scale * scale * scale * jnp.mean(weighted * acts, axis=-1, keepdims=True)
        gradacts_ref[...] = (gradresid_ref[...] + (scale * weighted - acts * slope)).astype(bf16)


def back_call(
    target, route, returned, up, resid, router, normed_two, mixed, tokens, gain_one,
    gain_two, wr, wo, wq, wk, wv, q, k, v, probs,
):
    length, width = tokens.shape
    rows = returned.shape[0]
    experts = wr.shape[1]
    part = GROUP * HEAD
    whole = lambda *shape: pl.BlockSpec(shape, lambda g: (0,) * len(shape))
    columns = lambda size: pl.BlockSpec((size, part), lambda g: (0, g))
    shape = jax.ShapeDtypeStruct
    return pl.pallas_call(
        back_kernel,
        grid=(HEADS // GROUP,),
        in_specs=[
            whole(length, 2), whole(length, 1), whole(rows, width),
            whole(length, width), whole(length, width), whole(length, experts),
            whole(length, width), whole(length, width), whole(length, width),
            whole(1, width), whole(1, width), whole(width, experts), whole(width, width),
            columns(width), columns(width), columns(width),
            columns(length), columns(length), columns(length),
            pl.BlockSpec((GROUP, length, length), lambda g: (g, 0, 0)),
        ],
        out_specs=[
            whole(length, width), whole(length, width),
            pl.BlockSpec((GROUP, BLOCK, 2 * length), lambda g: (g, 0, 0)),
            columns(width), columns(width), columns(width), whole(width, width),
            whole(width, experts), whole(2, width), whole(1, experts),
        ],
        out_shape=[
            shape((length, width), bf16), shape((length, width), bf16),
            shape((HEADS, BLOCK, 2 * length), f32),
            shape((width, width), f32), shape((width, width), f32), shape((width, width), f32),
            shape((width, width), f32), shape((width, experts), f32), shape((2, width), f32),
            shape((1, experts), f32),
        ],
        scratch_shapes=[
            pltpu.VMEM((width // part, length, part), bf16),
            pltpu.VMEM((length, width), f32),
            pltpu.VMEM((width, length), bf16),
            pltpu.VMEM((length, width), f32),
            pltpu.VMEM((width // part, length, part), f32),
        ],
        compiler_params=params(),
        cost_estimate=pl.CostEstimate(
            flops=2 * length * width * width * 8 + 8 * length * length * width * 4,
            bytes_accessed=30 * 1024 * 1024, transcendentals=0,
        ),
        name="back",
    )(
        target, route, returned, up, resid, router, normed_two, mixed, tokens, gain_one,
        gain_two, wr, wo, wq, wk, wv, q, k, v, probs,
    )


def skew_kernel(lines_ref, out_ref):
    heads, block, span = out_ref.shape
    for head in range(heads):
        row = jnp.broadcast_to(lines_ref[head : head + 1, :], (block, span))
        out_ref[head] = pltpu.roll(row, span - (block - 1), 1, stride=1, stride_axis=0)


def skew_call(lines, block):
    heads, span = lines.shape
    return pl.pallas_call(
        skew_kernel,
        out_shape=jax.ShapeDtypeStruct((heads, block, span), f32),
        compiler_params=params(),
        name="skew",
    )(lines)


def exchange(buffer):
    return lax.all_to_all(buffer, AXES, split_axis=0, concat_axis=0, tiled=True)


def swap(value, bit):
    devices = lax.axis_size(AXES)
    return lax.ppermute(value, AXES, [(at, at ^ (1 << bit)) for at in range(devices)])


def own_bit(bit):
    return ((lax.axis_index(AXES) >> bit) & 1) == 1


def gather_step(held, bit):
    value, done = held
    theirs = swap(value, bit)
    upper = own_bit(bit)
    place = sum(1 for other in done if other > bit)
    value = jnp.stack(
        [jnp.where(upper, theirs, value), jnp.where(upper, value, theirs)], axis=place
    )
    return value, done + [bit]


def gather_all(value, order):
    held = (value, [])
    for bit in order:
        held = gather_step(held, bit)
    return held[0].reshape((-1,) + value.shape)


def scatter_all(parts, order):
    bits = len(order)
    held = parts.reshape((2,) * bits + parts.shape[1:])
    left = list(range(bits))[::-1]
    for bit in order:
        place = left.index(bit)
        low = lax.index_in_dim(held, 0, place, keepdims=False)
        high = lax.index_in_dim(held, 1, place, keepdims=False)
        upper = own_bit(bit)
        sent = jnp.where(upper, low, high).astype(bf16)
        held = jnp.where(upper, high, low) + swap(sent, bit).astype(f32)
        left.remove(bit)
    return held


def pack_rows(parts, width):
    lead = parts[0].shape[0]
    flat = jnp.concatenate([part.reshape(lead, -1) for part in parts], axis=1)
    short = -flat.shape[1] % width
    return jnp.pad(flat, ((0, 0), (0, short))).reshape(lead, -1, width)


def unpack_rows(packed, sizes):
    flat = packed.reshape(packed.shape[0], -1)
    out, at = [], 0
    for size in sizes:
        out.append(flat[:, at : at + size])
        at += size
    return out


def body(
    tokens,
    w_query,
    w_key,
    w_value,
    w_output,
    w_router,
    gain_attn,
    gain_ffn,
    rel_bias,
    router_bias,
    w_in,
    w_out,
    routes,
    fill_rank,
    bucket_map,
    upstream_grad,
):
    batches, length, width = tokens.shape
    devices = lax.axis_size(AXES)
    wide_bits = lax.axis_size("wide").bit_length() - 1
    bits = devices.bit_length() - 1
    local_experts = w_in.shape[0]
    experts = local_experts * devices
    capacity = max(2, 5 * length // (4 * experts))
    slots = experts * capacity
    span = 2 * length
    far = list(range(wide_bits, bits))
    near = list(range(1, wide_bits))
    turned = near[1:] + near[:1]

    expert_ids = jnp.arange(experts, dtype=jnp.int32)

    def plan(at):
        route = routes[at, :, 0]
        order = fill_rank[at]
        route_hot = (route[:, None] == expert_ids[None, :]).astype(f32)
        earlier = (order[None, :] < order[:, None]).astype(bf16)
        counts = jnp.dot(earlier, route_hot.astype(bf16), preferred_element_type=f32)
        slot = jnp.sum(counts * route_hot, axis=-1).astype(jnp.int32)
        first = jnp.where(slot < capacity, route * (2 * capacity) + slot, -1)
        second = jnp.where(first >= 0, first + capacity, -1)
        return jnp.stack([first, second], axis=0)

    spots = [plan(at) for at in range(batches)]
    raw_spots = jnp.concatenate([spots[at][at] for at in range(batches)], axis=0)
    raw_ids = jnp.arange(2 * slots, dtype=jnp.int32)
    raw_sent = jnp.dot(
        (raw_ids[:, None] == raw_spots[None, :]).astype(bf16),
        upstream_grad.reshape(batches * length, width),
        preferred_element_type=f32,
    ).astype(bf16)

    small_parts = [w_router, gain_attn, gain_ffn, rel_bias, router_bias]
    small = pack_rows([part.reshape(1, -1) for part in small_parts], width)[0]
    small_all = gather_all(small, far[::-1] + near[::-1] + [0])
    wr_all, gain_one, gain_two, rel_flat, bias_all = unpack_rows(
        small_all, [part.size for part in small_parts]
    )
    wr_all = wr_all.reshape(width, experts)
    gain_one = gain_one.reshape(1, width).astype(f32)
    gain_two = gain_two.reshape(1, width).astype(f32)
    bias_all = bias_all.reshape(1, experts).astype(f32)
    table = rel_flat.reshape(BUCKETS, HEADS).T
    bucket_hot = (
        jnp.arange(BUCKETS, dtype=jnp.int32)[:, None]
        == jnp.pad(bucket_map, (0, 1), constant_values=-1)[None, :]
    ).astype(bf16)
    skewed = skew_call(jnp.dot(table, bucket_hot, preferred_element_type=f32), BLOCK)

    shard = w_query.shape[0]
    first_half = gather_all(
        jnp.concatenate([w_query, w_key], axis=0), far[::-1] + near[::-1] + [0]
    )
    second_half = gather_all(
        jnp.concatenate([w_value, w_output], axis=0), far[::-1] + turned[::-1] + [0]
    )
    wq, wk = (first_half[:, i * shard : (i + 1) * shard].reshape(width, width) for i in range(2))
    wv, wo = (second_half[:, i * shard : (i + 1) * shard].reshape(width, width) for i in range(2))

    raw_arrived = exchange(raw_sent.reshape(devices, 2 * capacity, width))

    own = lax.axis_index(AXES).astype(jnp.int32).reshape(1)
    row = jnp.arange(slots, dtype=jnp.int32)
    place = row + (row // capacity) * capacity
    place = jnp.stack([place, place + capacity], axis=1)

    fronts, arrived, returned, saved = [], [], [], []
    for at in range(batches):
        acts = tokens[at]
        if at == 1:
            acts, raw_arrived = lax.optimization_barrier((acts, raw_arrived))
        front = front_call(
            acts, wq, wk, wv, wo, skewed, gain_one, gain_two, wr_all, bias_all, spots[at], slots
        )
        fronts.append(front)
        arrived.append(exchange(front[-1].reshape(devices, 2 * capacity, width // 2)))
    raw = raw_arrived.reshape(devices, 2, capacity, width)
    for at in range(batches):
        held = expert_call(
            own,
            arrived[at].reshape(2 * slots, width // 2),
            raw[:, at].reshape(slots, width),
            wr_all,
            bias_all,
            place,
            w_in[0],
            w_out[0],
        )
        returned.append(exchange(held[0].reshape(devices, 2 * capacity, width)))
        saved.append(held[1:])

    grad_in = sum(
        jnp.einsum("rd,rf->df", rows, grad_inner, preferred_element_type=f32)
        for rows, active, grad_inner, grad_result in saved
    )
    grad_out = sum(
        jnp.einsum("rf,rd->fd", active, grad_result, preferred_element_type=f32)
        for rows, active, grad_inner, grad_result in saved
    )

    backs = []
    for at in range(batches):
        q, k, v, probs, mixed, resid, normed_two, router, sent = fronts[at]
        backs.append(
            back_call(
                spots[at].T,
                routes[at],
                returned[at].reshape(2 * slots, width),
                upstream_grad[at],
                resid,
                router,
                normed_two,
                mixed,
                tokens[at],
                gain_one,
                gain_two,
                wr_all,
                wo,
                wq,
                wk,
                wv,
                q,
                k,
                v,
                probs,
            )
        )
    folded, g_query, g_key, g_value, g_output, g_router, g_gains, g_bias = (
        sum(back[i] for back in backs) for i in range(2, 10)
    )
    rows = BLOCK
    while rows > 1:
        rows //= 2
        folded = folded[:, :rows] + jnp.roll(folded[:, rows:], -rows, axis=2)
    diagonal = jnp.roll(folded[:, 0], BLOCK - 1, axis=1)
    g_rel = jnp.einsum(
        "hn,bn->bh", diagonal, bucket_hot.astype(f32), precision=lax.Precision.HIGHEST
    )

    def parted(value):
        return value.reshape(devices, -1, width)

    small_grads = [g_router, g_gains[0], g_gains[1], g_rel, g_bias]
    small_pack = pack_rows([part.reshape(devices, -1) for part in small_grads], width)
    low = scatter_all(
        jnp.concatenate([parted(g_query), parted(g_key)], axis=1), [0] + near + far
    )
    high = scatter_all(
        jnp.concatenate([parted(g_value), parted(g_output)], axis=1), [0] + turned + far
    )
    small_sum = scatter_all(small_pack, [0] + near + far)
    tail = unpack_rows(small_sum[None], [part.size // devices for part in small_grads])
    r_router, r_gain_one, r_gain_two, r_rel, r_bias = (
        part.reshape(shape)
        for part, shape in zip(
            tail,
            (w_router.shape, gain_attn.shape, gain_ffn.shape, rel_bias.shape, router_bias.shape),
        )
    )
    return (
        jnp.stack([back[0] for back in backs], axis=0),
        jnp.stack([back[1] for back in backs], axis=0),
        low[:shard],
        low[shard:],
        high[:shard],
        high[shard:],
        r_router,
        r_gain_one,
        r_gain_two,
        r_rel,
        r_bias,
        grad_in[None],
        grad_out[None],
    )


def solution(mesh):
    both = P(AXES)
    in_specs = (both,) * 14 + (P(), both)
    out_specs = (both,) * 13
    return jax.shard_map(body, mesh=mesh, in_specs=in_specs, out_specs=out_specs, check_vma=False)
```

time: 644 us -> 415 us (0.64)
  matrix products: 229 us -> 35.1 us
  Pallas kernels: 5.3 us -> 148 us
  waiting for transfers between devices: 206 us -> 91.8 us
  local copies, waits for them, and re-layouts: 96.7 us -> 45.1 us
  starting transfers between devices: 25.8 us -> 58.6 us
  other arithmetic: 54.7 us -> 29.1 us
  between operations: 16.6 us -> 2.72 us
    dot_general x61 -> x2, matrix products: 206 us -> 5.98 us  [the longest x1 5.1 us: body(): jnp.dot((raw_ids[:, None] == raw_spots[None, :]).astype(bf16), upstream_g...]
    pallas_call x1 -> x7, Pallas kernels: 5.3 us -> 148 us  [the longest x2 55.5 us: back_call(): pl.pallas_call(back_kernel, grid=(HEADS // GROUP,), in_specs=[whole(lengt...]
    all_to_all x6 -> x5, waiting for transfers between devices: 99.5 us -> 10.9 us  [exchange(): return lax.all_to_all(buffer, AXES, split_axis=0, concat_axis=0, tiled=True)]
    ppermute x0 -> x30, waiting for transfers between devices: none -> 80.9 us  [swap(): lax.ppermute(value, AXES, [(at, at ^ 1 << bit) for at in range(devices)])]
    all_gather x1 -> x0, waiting for transfers between devices: 62.7 us -> none  [body(): everything = lax.all_gather(square, AXES, axis=0)]
    reduce_scatter x2 -> x0, waiting for transfers between devices: 43.9 us -> none  [the longest x1 35.8 us: body(): lax.psum_scatter(packed.reshape(narrow, wide, depth, width), 'wide', scat...]
    ppermute x0 -> x30, starting transfers between devices: none -> 37.4 us  [swap(): lax.ppermute(value, AXES, [(at, at ^ 1 << bit) for at in range(devices)])]
    convert_element_type x12 -> x19, other arithmetic: 21.6 us -> 3.38 us  [the longest x15 2.6 us: scatter_all(): sent = jnp.where(upper, low, high).astype(bf16)]
  transfers between devices with their start and end apart: 9 -> 35, of which waited for: 8 -> 21; matrix products, arithmetic and copies ran while one was open for 25% -> 21% of each run, Pallas kernels for 0% -> 29%
where the time goes in v2:
time: 415 us; the launch traced here: 411 us
  Pallas kernels  148 us (36%)
  waiting for transfers between devices  91.8 us (22%)
  starting transfers between devices  58.6 us (14%)
  local copies, waits for them, and re-layouts  45.1 us (11%)
  matrix products  35.1 us (8%)
  other arithmetic  29.1 us (7%)
    ppermute x30, waiting for transfers between devices, swap(): lax.ppermute(value, AXES, [(at, at ^ 1 << bit) for at in range(devices)])  80.9 us
    pallas_call x2, Pallas kernels, back_call(): pl.pallas_call(back_kernel, grid=(HEADS // GROUP,), in_specs=[whole(lengt...  55.5 us
    pallas_call x2, Pallas kernels, expert_call(): pl.pallas_call(expert_kernel, grid_spec=pltpu.PrefetchScalarGridSpec(num_...  52.1 us
    ppermute x30, starting transfers between devices, swap(): lax.ppermute(value, AXES, [(at, at ^ 1 << bit) for at in range(devices)])  37.4 us
    pallas_call x2, Pallas kernels, front_call(): pl.pallas_call(front_kernel, grid=(HEADS // GROUP,), in_specs=[whole(leng...  35.6 us
    all_to_all x5, starting transfers between devices, exchange(): return lax.all_to_all(buffer, AXES, split_axis=0, concat_axis=0, tiled=True)  21.2 us
    dot_general x2, matrix products, body(): jnp.einsum('rd,rf->df', rows, grad_inner, preferred_element_type=f32)  14.9 us
    unnamed x89, local copies, waits for them, and re-layouts  14 us
  transfers between devices with their start and end apart: 35, of which 21 were waited for; matrix products, arithmetic and copies ran while one was open for 21% of the time, Pallas kernels for 29%

profile of v2, /device:TPU:0, one launch (start us, length us, event | category | flops | bytes accessed | tf_op | source)
XLA Modules:
  0.0 410.9 jit_solution(10400979709554293992)
XLA Ops:
  2.9 4.1 collective-permute-start.10
  18.5 5.1 %fusion.1 = bf16[1280,768]{1,0:T(8,128)(2,1)} fusion(bf16[1024,768]{1,0:T(8,128)(2,1)} %bitcast.334, s32[1024]{0:T(1024)S(1)} %pad_add_fusion.2), kind=kOutput, calls=%fused_computation.8 | convolution fusion | flops 2015559680 | bytes 3543040 | tf_op jit(solution)/shard_map/dot_general | solution.py:540
  31.6 29.1 %collective-permute-done.11 = bf16[2,2,768]{2,1,0:T(2,128)(2,1)S(1)} collective-permute-done((bf16[2,2,768]{2,1,0:T(2,128)(2,1)S(1)}, bf16[2,2,768]{2,1,0:T(2,128)(2,1)S(1)}, u32[]{:S(2)}, u32[]{:S(2)}) %collective-permute-start.11) | collective-permute-done | bytes 6176 | tf_op jit(solution)/shard_map/ppermute | solution.py:437
  69.5 6.1 %collective-permute-done.6 = bf16[2,48,768]{2,1,0:T(8,128)(2,1)S(1)} collective-permute-done((bf16[2,48,768]{2,1,0:T(8,128)(2,1)S(1)}, bf16[2,48,768]{2,1,0:T(8,128)(2,1)S(1)}, u32[]{:S(2)}, u32[]{:S(2)}) %collective-permute-start.6) | collective-permute-done | bytes 147488 | tf_op jit(solution)/shard_map/ppermute | solution.py:437
  78.6 4.7 %collective-permute-done.7 = bf16[2,2,48,768]{3,2,0,1:T(8,128)(2,1)S(1)} collective-permute-done((bf16[2,2,48,768]{3,2,0,1:T(8,128)(2,1)S(1)}, bf16[2,2,48,768]{3,2,0,1:T(8,128)(2,1)S(1)}, u32[]{:S(2)}, u32[]{:S(2)}) %collective-permute-start.7) | collective-permute-done | bytes 294944 | tf_op jit(solution)/shard_map/ppermute | solution.py:437
  83.4 4.6 %collective-permute-done.2 = bf16[2,2,48,768]{3,2,1,0:T(8,128)(2,1)S(1)} collective-permute-done((bf16[2,2,48,768]{3,2,1,0:T(8,128)(2,1)S(1)}, bf16[2,2,48,768]{3,2,1,0:T(8,128)(2,1)S(1)}, u32[]{:S(2)}, u32[]{:S(2)}) %collective-permute-start.2) | collective-permute-done | bytes 294944 | tf_op jit(solution)/shard_map/ppermute | solution.py:437
  89.1 10.0 %collective-permute-done.8 = bf16[2,2,2,48,768]{4,3,0,1,2:T(8,128)(2,1)S(1)} collective-permute-done((bf16[2,2,2,48,768]{4,3,0,1,2:T(8,128)(2,1)S(1)}, bf16[2,2,2,48,768]{4,3,0,1,2:T(8,128)(2,1)S(1)}, u32[]{:S(2)}, u32[]{:S(2)}) %collective-permute-start.8) | collective-permute-done | bytes 589856 | tf_op jit(solution)/shard_map/ppermute | solution.py:437
  106.3 5.2 %skew.1.skew_ref = f32[12,128,1024]{2,1,0:T(8,128)} custom-call(f32[12,1024]{1,0:T(8,128)} %fusion.24.lines_ref), custom_call_target="tpu_custom_call" | custom-call | tf_op jit(solution)/shard_map/skew/pallas_call | solution.py:423
  120.0 17.8 %front.2 = (bf16[512,768]{1,0:T(8,128)(2,1)}, bf16[512,768]{1,0:T(8,128)(2,1)}, bf16[512,768]{1,0:T(8,128)(2,1)}, bf16[12,512,512]{2,1,0:T(8,128)(2,1)}, bf16[51...) custom-call(bf16[512,768]{1,0:T(8,128)(2,1)} %get-tuple-element.135., ...), custom_call_target="tpu_custom_call" | custom-call | flops 5637144576 | bytes 26214400 | tf_op jit(solution)/shard_map/front/pallas_call | solution.py:110
  141.0 17.8 %front.3 = (bf16[512,768]{1,0:T(8,128)(2,1)}, bf16[512,768]{1,0:T(8,128)(2,1)}, bf16[512,768]{1,0:T(8,128)(2,1)}, bf16[12,512,512]{2,1,0:T(8,128)(2,1)}, bf16[51...) custom-call(bf16[512,768]{1,0:T(8,128)(2,1)} %get-tuple-element.75.t, ...), custom_call_target="tpu_custom_call" | custom-call | flops 5637144576 | bytes 26214400 | tf_op jit(solution)/shard_map/front/pallas_call | solution.py:110
  158.8 7.0 %all-to-all-done = bf16[32,40,384]{2,1,0:T(8,128)(2,1)S(1)} async-done(((bf16[32,40,384]{2,1,0:T(8,128)(2,1)}), bf16[32,40,384]{2,1,0:T(8,128)(2,1)S(1)}, u32[]{:S(2)}, u32[]{:S(2)}) %all-to-all-start) | async-done | bytes 983072 | tf_op jit(solution)/shard_map/all_to_all | solution.py:432
  174.2 26.1 %expert.2 = (bf16[1280,768]{1,0:T(8,128)(2,1)}, bf16[640,768]{1,0:T(8,128)(2,1)}, bf16[640,3072]{1,0:T(8,128)(2,1)}, bf16[640,3072]{1,0:T(8,128)(2,1)}, bf16[640,768]{1,0:T(8,128)(2,1)}) custom-call(s32[1]{0:T(128)} %bitcast.6.own_ref, bf16[1280,384]{1,0:T(8,128)(2,1)} %bitcast.352, bf16[640,768]{1,0:T(8,128)(2,1)} %reshape_squeeze.12.raw_ref, ...), custom_call_target="tpu_custom_call" | custom-call | flops 12079595520 | bytes 20971520 | tf_op jit(solution)/shard_map/expert/pallas_call | solution.py:215
  200.3 6.1 %all-to-all-start.2 = ((bf16[32,40,768]{2,1,0:T(8,128)(2,1)}), bf16[32,40,768]{2,1,0:T(8,128)(2,1)}, u32[]{:S(2)}, u32[]{:S(2)}) async-start(bf16[32,40,768]{2,1,0:T(8,128)(2,1)} %bitcast.333), calls=%async_computation.2 | async-start | bytes 3932160 | tf_op jit(solution)/shard_map/all_to_all | solution.py:432
  214.2 8.4 %fusion.72 = f32[768,3072]{1,0:T(8,128)} fusion(bf16[640,768]{1,0:T(8,128)(2,1)S(1)} %copy-done.18, bf16[640,3072]{1,0:T(8,128)(2,1)} %get-tuple-element.106), kind=kOutput, calls=%fused_computation.213 | convolution fusion | flops 3019898880 | bytes 14352384 | tf_op jit(solution)/shard_map/rd,rf->df/dot_general | solution.py:606
  222.5 26.1 %expert.3 = (bf16[1280,768]{1,0:T(8,128)(2,1)}, bf16[640,768]{1,0:T(8,128)(2,1)}, bf16[640,3072]{1,0:T(8,128)(2,1)}, bf16[640,3072]{1,0:T(8,128)(2,1)}, bf16[640,768]{1,0:T(8,128)(2,1)}) custom-call(s32[1]{0:T(128)} %bitcast.6.own_ref, bf16[1280,384]{1,0:T(8,128)(2,1)} %bitcast.351, bf16[640,768]{1,0:T(8,128)(2,1)} %reshape_squeeze.13.raw_ref, ...), custom_call_target="tpu_custom_call" | custom-call | flops 12079595520 | bytes 20971520 | tf_op jit(solution)/shard_map/expert/pallas_call | solution.py:215
  252.5 4.2 %all-to-all-start.4 = ((bf16[32,40,768]{2,1,0:T(8,128)(2,1)}), bf16[32,40,768]{2,1,0:T(8,128)(2,1)S(1)}, u32[]{:S(2)}, u32[]{:S(2)}) async-start(bf16[32,40,768]{2,1,0:T(8,128)(2,1)} %bitcast.332), calls=%async_computation.4 | async-start | bytes 3932160 | tf_op jit(solution)/shard_map/all_to_all | solution.py:432
  256.8 6.5 %fusion.73 = f32[3072,768]{1,0:T(8,128)S(1)} fusion(bf16[640,3072]{1,0:T(8,128)(2,1)} %get-tuple-element.109, bf16[640,768]{1,0:T(8,128)(2,1)} %get-tuple-element.110), kind=kOutput, calls=%fused_computation.214 | convolution fusion | flops 3019898880 | bytes 14352384 | tf_op jit(solution)/shard_map/rf,rd->fd/dot_general | solution.py:610
  263.3 6.6 %add_bitcast_fusion = f32[1,3072,768]{2,1,0:T(8,128)} fusion(f32[3072,768]{1,0:T(8,128)S(1)} %fusion.73, bf16[640,3072]{1,0:T(8,128)(2,1)S(1)} %copy-done.37, bf16[640,768]{1,0:T(8,128)(2,1)S(1)} %copy-done.38), kind=kOutput, calls=%fused_computation | convolution fusion | flops 3022258176 | bytes 23789568 | tf_op jit(solution)/shard_map/rf,rd->fd/dot_general | solution.py:610
  270.0 6.5 %add_bitcast_fusion.1 = f32[1,768,3072]{2,1,0:T(8,128)} fusion(f32[768,3072]{1,0:T(8,128)S(1)} %bitcast.322, bf16[640,768]{1,0:T(8,128)(2,1)S(1)} %copy-done.19, bf16[640,3072]{1,0:T(8,128)(2,1)S(1)} %copy-done.6), kind=kOutput, calls=%fused_computation.1 | convolution fusion | flops 3022258176 | bytes 23789568 | tf_op jit(solution)/shard_map/rd,rf->df/dot_general | solution.py:606
  276.5 27.7 %back.2 = (bf16[512,768]{1,0:T(8,128)(2,1)}, bf16[512,768]{1,0:T(8,128)(2,1)}, f32[12,128,1024]{2,1,0:T(8,128)}, f32[768,768]{1,0:T(8,128)}, f32[768,768]{1,0:T(...) custom-call(s32[512,2]{1,0:T(8,128)} %bitcast.365, ...), custom_call_target="tpu_custom_call" | custom-call | flops 11274289152 | bytes 31457280 | tf_op jit(solution)/shard_map/back/pallas_call | solution.py:370
  305.5 27.8 %back.3 = (bf16[512,768]{1,0:T(8,128)(2,1)}, bf16[512,768]{1,0:T(8,128)(2,1)}, f32[12,128,1024]{2,1,0:T(8,128)}, f32[768,768]{1,0:T(8,128)}, f32[768,768]{1,0:T(...) custom-call(s32[512,2]{1,0:T(8,128)} %bitcast.364, ...), custom_call_target="tpu_custom_call" | custom-call | flops 11274289152 | bytes 31457280 | tf_op jit(solution)/shard_map/back/pallas_call | solution.py:370
  333.3 6.1 %add.253 = f32[12,128,1024]{2,1,0:T(8,128)S(1)} add(f32[12,128,1024]{2,1,0:T(8,128)} %get-tuple-element.101, f32[12,128,1024]{2,1,0:T(8,128)} %get-tuple-element.102) | non-fusion elementwise | flops 1572864 | bytes 18874368 | tf_op jit(solution)/shard_map/add | solution.py:642
  380.2 4.9 %collective-permute-done.16 = bf16[2,2,2,48,768]{4,3,0,1,2:T(8,128)(2,1)S(1)} collective-permute-done((bf16[2,2,2,48,768]{4,3,0,1,2:T(8,128)(2,1)}, bf16[2,2,2,48,768]{4,3,0,1,2:T(8,128)(2,1)S(1)}, u32[]{:S(2)}, u32[]{:S(2)}) %collective-permute-start.16) | collective-permute-done | bytes 589856 | tf_op jit(solution)/shard_map/ppermute | solution.py:437
  386.3 5.8 %collective-permute-done.21 = bf16[2,2,2,48,768]{4,3,0,1,2:T(8,128)(2,1)S(1)} collective-permute-done((bf16[2,2,2,48,768]{4,3,0,1,2:T(8,128)(2,1)}, bf16[2,2,2,48,768]{4,3,0,1,2:T(8,128)(2,1)S(1)}, u32[]{:S(2)}, u32[]{:S(2)}) %collective-permute-start.21) | collective-permute-done | bytes 589856 | tf_op jit(solution)/shard_map/ppermute | solution.py:437
  (300 shorter events, 133.9 us)
Async XLA Ops:
  2.9 26.0 %collective-permute-start.10 = (bf16[2,768]{1,0:T(2,128)(2,1)S(1)}, bf16[2,768]{1,0:T(2,128)(2,1)}, u32[]{:S(2)}, u32[]{:S(2)}) collective-permute-start(bf16[2,768]{1,0:T(2,128)(2,1)S(1)} %squeeze_reshape.3), channel_id=1, source_target_pairs={{0,16},{1,17},{2,18},{3,19},{4,20},{5,21},{6,22},{7,23},{8,24},{9,... | collective-permute-start | bytes 9224 | tf_op jit(solution)/shard_map/ppermute | solution.py:437
  9.8 54.9 %collective-permute-start.5 = (bf16[48,768]{1,0:T(8,128)(2,1)}, bf16[48,768]{1,0:T(8,128)(2,1)}, u32[]{:S(2)}, u32[]{:S(2)}) collective-permute-start(bf16[48,768]{1,0:T(8,128)(2,1)} %constant_dynamic-update-slice_fusion.2), channel_id=1, source_target_pairs={{0,16},{1,17},{2,18},{3,19},{4,20},{5,21},{6,22},{7,23},{8,24},{9,... | collective-permute-start | bytes 221192 | tf_op jit(solution)/shard_map/ppermute | solution.py:437
  12.6 52.2 %collective-permute-start = (bf16[48,768]{1,0:T(8,128)(2,1)}, bf16[48,768]{1,0:T(8,128)(2,1)}, u32[]{:S(2)}, u32[]{:S(2)}) collective-permute-start(bf16[48,768]{1,0:T(8,128)(2,1)} %constant_dynamic-update-slice_fusion), channel_id=1, source_target_pairs={{0,16},{1,17},{2,18},{3,19},{4,20},{5,21},{6,22},{7,23},{8,24},{9,... | collective-permute-start | bytes 221192 | tf_op jit(solution)/shard_map/ppermute | solution.py:437
  23.6 114.2 %all-to-all-start.1 = ((bf16[32,40,768]{2,1,0:T(8,128)(2,1)}), bf16[32,40,768]{2,1,0:T(8,128)(2,1)S(1)}, u32[]{:S(2)}, u32[]{:S(2)}) async-start(bf16[32,40,768]{2,1,0:T(8,128)(2,1)} %bitcast.330), calls=%async_computation.1 | async-start | bytes 3932160 | tf_op jit(solution)/shard_map/all_to_all | solution.py:432
  29.7 31.1 %collective-permute-start.11 = (bf16[2,2,768]{2,1,0:T(2,128)(2,1)S(1)}, bf16[2,2,768]{2,1,0:T(2,128)(2,1)S(1)}, u32[]{:S(2)}, u32[]{:S(2)}) collective-permute-start(bf16[2,2,768]{2,1,0:T(2,128)(2,1)S(1)} %pad_maximum_fusion.18), channel_id=1, source_target_pairs={{0,8},{1,9},{2,10},{3,11},{4,12},{5,13},{6,14},{7,15},{8,0},{9,1},... | collective-permute-start | bytes 18440 | tf_op jit(solution)/shard_map/ppermute | solution.py:437
  65.8 9.8 %collective-permute-start.6 = (bf16[2,48,768]{2,1,0:T(8,128)(2,1)S(1)}, bf16[2,48,768]{2,1,0:T(8,128)(2,1)S(1)}, u32[]{:S(2)}, u32[]{:S(2)}) collective-permute-start(bf16[2,48,768]{2,1,0:T(8,128)(2,1)S(1)} %pad_maximum_fusion.13), channel_id=1, source_target_pairs={{0,8},{1,9},{2,10},{3,11},{4,12},{5,13},{6,14},{7,15},{8,0},{9,1},... | collective-permute-start | bytes 442376 | tf_op jit(solution)/shard_map/ppermute | solution.py:437
  68.2 20.7 %collective-permute-start.13 = (bf16[2,2,2,2,768]{4,3,0,1,2:T(2,128)(2,1)S(1)}, bf16[2,2,2,2,768]{4,3,0,1,2:T(2,128)(2,1)S(1)}, u32[]{:S(2)}, u32[]{:S(2)}) collective-permute-start(bf16[2,2,2,2,768]{4,3,0,1,2:T(2,128)(2,1)S(1)} %pad_maximum_fusion.16), channel_id=1, source_target_pairs={{0,2},{1,3},{2,0},{3,1},{4,6},{5,7},{6,4},{7,5},{8,10},{9,11},{10,... | collective-permute-start | bytes 73736 | tf_op jit(solution)/shard_map/ppermute | solution.py:437
  69.4 8.6 %collective-permute-start.1 = (bf16[2,48,768]{2,1,0:T(8,128)(2,1)S(1)}, bf16[2,48,768]{2,1,0:T(8,128)(2,1)S(1)}, u32[]{:S(2)}, u32[]{:S(2)}) collective-permute-start(bf16[2,48,768]{2,1,0:T(8,128)(2,1)S(1)} %pad_maximum_fusion.12), channel_id=1, source_target_pairs={{0,8},{1,9},{2,10},{3,11},{4,12},{5,13},{6,14},{7,15},{8,0},{9,1},... | collective-permute-start | bytes 442376 | tf_op jit(solution)/shard_map/ppermute | solution.py:437
  78.1 10.0 %collective-permute-start.2 = (bf16[2,2,48,768]{3,2,1,0:T(8,128)(2,1)S(1)}, bf16[2,2,48,768]{3,2,1,0:T(8,128)(2,1)S(1)}, u32[]{:S(2)}, u32[]{:S(2)}) collective-permute-start(bf16[2,2,48,768]{3,2,1,0:T(8,128)(2,1)S(1)} %pad_maximum_fusion.10), channel_id=1, source_target_pairs={{0,4},{1,5},{2,6},{3,7},{4,0},{5,1},{6,2},{7,3},{8,12},{9,13},{10,... | collective-permute-start | bytes 884744 | tf_op jit(solution)/shard_map/ppermute | solution.py:437
  83.4 15.7 %collective-permute-start.8 = (bf16[2,2,2,48,768]{4,3,0,1,2:T(8,128)(2,1)S(1)}, bf16[2,2,2,48,768]{4,3,0,1,2:T(8,128)(2,1)S(1)}, u32[]{:S(2)}, u32[]{:S(2)}) collective-permute-start(bf16[2,2,2,48,768]{4,3,0,1,2:T(8,128)(2,1)S(1)} %pad_maximum_fusion.9), channel_id=1, source_target_pairs={{0,4},{1,5},{2,6},{3,7},{4,0},{5,1},{6,2},{7,3},{8,12},{9,13},{10,... | collective-permute-start | bytes 1769480 | tf_op jit(solution)/shard_map/ppermute | solution.py:437
  88.2 12.1 %collective-permute-start.3 = (bf16[2,2,2,48,768]{4,3,2,1,0:T(8,128)(2,1)S(1)}, bf16[2,2,2,48,768]{4,3,2,1,0:T(8,128)(2,1)S(1)}, u32[]{:S(2)}, u32[]{:S(2)}) collective-permute-start(bf16[2,2,2,48,768]{4,3,2,1,0:T(8,128)(2,1)S(1)} %pad_maximum_fusion.8), channel_id=1, source_target_pairs={{0,2},{1,3},{2,0},{3,1},{4,6},{5,7},{6,4},{7,5},{8,10},{9,11},{10,... | collective-permute-start | bytes 1769480 | tf_op jit(solution)/shard_map/ppermute | solution.py:437
  89.0 13.8 %collective-permute-start.14 = (bf16[2,2,2,2,2,768]{5,4,0,1,2,3:T(2,128)(2,1)S(1)}, bf16[2,2,2,2,2,768]{5,4,0,1,2,3:T(2,128)(2,1)S(1)}, u32[]{:S(2)}, u32[]{:S(2)}) collective-permute-start(bf16[2,2,2,2,2,768]{5,4,0,1,2,3:T(2,128)(2,1)S(1)} %pad_maximum_fusion.15), channel_id=1, source_target_pairs={{0,1},{1,0},{2,3},{3,2},{4,5},{5,4},{6,7},{7,6},{8,9},{9,8},{10,11... | collective-permute-start | bytes 147464 | tf_op jit(solution)/shard_map/ppermute | solution.py:437
  100.3 12.0 %collective-permute-start.9 = (bf16[2,2,2,2,48,768]{5,4,0,1,3,2:T(8,128)(2,1)}, bf16[2,2,2,2,48,768]{5,4,0,1,3,2:T(8,128)(2,1)}, u32[]{:S(2)}, u32[]{:S(2)}) collective-permute-start(bf16[2,2,2,2,48,768]{5,4,0,1,3,2:T(8,128)(2,1)} %pad_maximum_fusion.7), channel_id=1, source_target_pairs={{0,1},{1,0},{2,3},{3,2},{4,5},{5,4},{6,7},{7,6},{8,9},{9,8},{10,11... | collective-permute-start | bytes 3538952 | tf_op jit(solution)/shard_map/ppermute | solution.py:437
  102.3 11.9 %collective-permute-start.4 = (bf16[2,2,2,2,48,768]{5,4,3,2,1,0:T(8,128)(2,1)}, bf16[2,2,2,2,48,768]{5,4,3,2,1,0:T(8,128)(2,1)}, u32[]{:S(2)}, u32[]{:S(2)}) collective-permute-start(bf16[2,2,2,2,48,768]{5,4,3,2,1,0:T(8,128)(2,1)} %pad_maximum_fusion.6), channel_id=1, source_target_pairs={{0,1},{1,0},{2,3},{3,2},{4,5},{5,4},{6,7},{7,6},{8,9},{9,8},{10,11... | collective-permute-start | bytes 3538952 | tf_op jit(solution)/shard_map/ppermute | solution.py:437
  137.8 28.0 %all-to-all-start = ((bf16[32,40,384]{2,1,0:T(8,128)(2,1)}), bf16[32,40,384]{2,1,0:T(8,128)(2,1)S(1)}, u32[]{:S(2)}, u32[]{:S(2)}) async-start(bf16[32,40,384]{2,1,0:T(8,128)(2,1)} %bitcast.354), calls=%async_computation | async-start | bytes 1966080 | tf_op jit(solution)/shard_map/all_to_all | solution.py:432
  166.8 33.5 %all-to-all-start.3 = ((bf16[32,40,384]{2,1,0:T(8,128)(2,1)}), bf16[32,40,384]{2,1,0:T(8,128)(2,1)S(1)}, u32[]{:S(2)}, u32[]{:S(2)}) async-start(bf16[32,40,384]{2,1,0:T(8,128)(2,1)} %bitcast.353), calls=%async_computation.3 | async-start | bytes 1966080 | tf_op jit(solution)/shard_map/all_to_all | solution.py:432
  200.3 52.2 %all-to-all-start.2 = ((bf16[32,40,768]{2,1,0:T(8,128)(2,1)}), bf16[32,40,768]{2,1,0:T(8,128)(2,1)}, u32[]{:S(2)}, u32[]{:S(2)}) async-start(bf16[32,40,768]{2,1,0:T(8,128)(2,1)} %bitcast.333), calls=%async_computation.2 | async-start | bytes 3932160 | tf_op jit(solution)/shard_map/all_to_all | solution.py:432
  252.5 51.8 %all-to-all-start.4 = ((bf16[32,40,768]{2,1,0:T(8,128)(2,1)}), bf16[32,40,768]{2,1,0:T(8,128)(2,1)S(1)}, u32[]{:S(2)}, u32[]{:S(2)}) async-start(bf16[32,40,768]{2,1,0:T(8,128)(2,1)} %bitcast.332), calls=%async_computation.4 | async-start | bytes 3932160 | tf_op jit(solution)/shard_map/all_to_all | solution.py:432
  344.8 9.5 %collective-permute-start.25 = (bf16[2,2,2,2,2,768]{5,4,3,2,1,0:T(2,128)(2,1)S(1)}, bf16[2,2,2,2,2,768]{5,4,3,2,1,0:T(2,128)(2,1)S(1)}, u32[]{:S(2)}, u32[]{:S(2)}) collective-permute-start(bf16[2,2,2,2,2,768]{5,4,3,2,1,0:T(2,128)(2,1)S(1)} %fusion.40), channel_id=1, source_target_pairs={{0,1},{1,0},{2,3},{3,2},{4,5},{5,4},{6,7},{7,6},{8,9},{9,8},{10,11... | collective-permute-start | bytes 147464 | tf_op jit(solution)/shard_map/ppermute | solution.py:437
  349.5 22.2 %collective-permute-start.15 = (bf16[2,2,2,2,48,768]{5,4,0,1,3,2:T(8,128)(2,1)S(1)}, bf16[2,2,2,2,48,768]{5,4,0,1,3,2:T(8,128)(2,1)S(1)}, u32[]{:S(2)}, u32[]{:S(2)}) collective-permute-start(bf16[2,2,2,2,48,768]{5,4,0,1,3,2:T(8,128)(2,1)S(1)} %fusion.5), channel_id=1, source_target_pairs={{0,1},{1,0},{2,3},{3,2},{4,5},{5,4},{6,7},{7,6},{8,9},{9,8},{10,11... | collective-permute-start | bytes 3538952 | tf_op jit(solution)/shard_map/ppermute | solution.py:437
  360.4 14.3 %collective-permute-start.20 = (bf16[2,2,2,2,48,768]{5,4,0,1,3,2:T(8,128)(2,1)S(1)}, bf16[2,2,2,2,48,768]{5,4,0,1,3,2:T(8,128)(2,1)S(1)}, u32[]{:S(2)}, u32[]{:S(2)}) collective-permute-start(bf16[2,2,2,2,48,768]{5,4,0,1,3,2:T(8,128)(2,1)S(1)} %fusion.6), channel_id=1, source_target_pairs={{0,1},{1,0},{2,3},{3,2},{4,5},{5,4},{6,7},{7,6},{8,9},{9,8},{10,11... | collective-permute-start | bytes 3538952 | tf_op jit(solution)/shard_map/ppermute | solution.py:437
  373.0 12.0 %collective-permute-start.16 = (bf16[2,2,2,48,768]{4,3,0,1,2:T(8,128)(2,1)}, bf16[2,2,2,48,768]{4,3,0,1,2:T(8,128)(2,1)S(1)}, u32[]{:S(2)}, u32[]{:S(2)}) collective-permute-start(bf16[2,2,2,48,768]{4,3,0,1,2:T(8,128)(2,1)} %fusion.13), channel_id=1, source_target_pairs={{0,2},{1,3},{2,0},{3,1},{4,6},{5,7},{6,4},{7,5},{8,10},{9,11},{10,... | collective-permute-start | bytes 1769480 | tf_op jit(solution)/shard_map/ppermute | solution.py:437
  377.4 14.7 %collective-permute-start.21 = (bf16[2,2,2,48,768]{4,3,0,1,2:T(8,128)(2,1)}, bf16[2,2,2,48,768]{4,3,0,1,2:T(8,128)(2,1)S(1)}, u32[]{:S(2)}, u32[]{:S(2)}) collective-permute-start(bf16[2,2,2,48,768]{4,3,0,1,2:T(8,128)(2,1)} %fusion.14), channel_id=1, source_target_pairs={{0,4},{1,5},{2,6},{3,7},{4,0},{5,1},{6,2},{7,3},{8,12},{9,13},{10,... | collective-permute-start | bytes 1769480 | tf_op jit(solution)/shard_map/ppermute | solution.py:437
  385.3 10.0 %collective-permute-start.17 = (bf16[2,2,48,768]{3,2,0,1:T(8,128)(2,1)S(1)}, bf16[2,2,48,768]{3,2,0,1:T(8,128)(2,1)S(1)}, u32[]{:S(2)}, u32[]{:S(2)}) collective-permute-start(bf16[2,2,48,768]{3,2,0,1:T(8,128)(2,1)S(1)} %fusion.19), channel_id=1, source_target_pairs={{0,4},{1,5},{2,6},{3,7},{4,0},{5,1},{6,2},{7,3},{8,12},{9,13},{10,... | collective-permute-start | bytes 884744 | tf_op jit(solution)/shard_map/ppermute | solution.py:437
  (53 other events, 218.7 us)
